TPU v7x, 32 devices: a whole 2x2x4 slice. The times are simulated.
32 devices in a mesh: section: 2 (over y), dp: 8 (over z, x), tensor: 2 (over core).
Axes of the slice: x: 2, y: 2, z: 4, core: 2. Of those that a mesh axis runs over, the one named last changes fastest.
Arguments:
- chain_inputs: bfloat16 [7680, 768], P('dp', 'tensor'), may hold values from -6 to 6
- cotangent: bfloat16 [7680, 768], P('dp', 'tensor'), may hold values from -6 to 6
- chain_tags: int32 [48], P('dp'), may hold values 0 or 1
- pad_mask: int32 [7680], P('dp'), may hold values from 0 to 1, as said below
- predicted: int32 [7680], P('dp'), may hold values from 0 to 23
- target_ids: int32 [7680], P('dp'), may hold values from 0 to 23
- joint_proj: bfloat16 [2, 2, 768, 3, 768], P('section', None, None, None, 'tensor'), may hold values from -0.21875 to 0.21875
- output_proj: bfloat16 [2, 2, 768, 768], P('section', None, 'tensor'), may hold values from -0.875 to 0.875
- up_proj: bfloat16 [2, 2, 768, 3072], P('section', None, None, 'tensor'), may hold values from -0.21875 to 0.21875
- up_bias: bfloat16 [2, 2, 3072], P('section', None, 'tensor'), may hold values from -3 to 3
- down_proj: bfloat16 [2, 2, 3072, 768], P('section', None, 'tensor'), may hold values from -0.109375 to 0.109375
- norm_gain: float32 [2, 2, 768], P('section'), may hold values from 0.25 to 1.75
- norm_shift: float32 [2, 2, 768], P('section'), may hold values from -2 to 2
Outputs:
- layer_outputs: bfloat16 [2, 7680, 768], P('section', 'dp', 'tensor')
- input_grads: float32 [2, 7680, 768], P('section', 'dp', 'tensor')
- joint_grad: float32 [2, 2, 768, 3, 768], P('section', None, None, None, 'tensor')
- output_grad: float32 [2, 2, 768, 768], P('section', None, 'tensor')
- up_grad: float32 [2, 2, 768, 3072], P('section', None, None, 'tensor')
- bias_grad: float32 [2, 2, 3072], P('section', None, 'tensor')
- down_grad: float32 [2, 2, 3072, 768], P('section', None, 'tensor')
- gain_grad: float32 [2, 2, 768], P('section')
- shift_grad: float32 [2, 2, 768], P('section')
- residue_counts: int32 [2, 24], replicated
Inputs may be any that keep to these rules, and one draw needn't show every extreme that they name: `pad_mask`: each chain's live positions are its first ones, at least 40 of them; some chains are padded.
All inputs are finite; a program needn't handle non-finite values. No bound on the sum of `chain_tags` on one device may be relied on, other than what follows from the above.
Results may differ from a plain program's by a relative error of at most 0.035.
Values may be sent and summed in bfloat16 or wider, within the bound.
No kernel may reach another device: no remote copies, remote signals or barrier semaphores. Data moves between devices by JAX's collectives and lax.ppermute only.
A program may use at most 256 MiB of HBM per device.

v0:
```python
import functools

import jax
import jax.numpy as jnp
from jax import lax
from jax.experimental import pallas as pl
from jax.experimental.pallas import tpu as pltpu
from jax.sharding import PartitionSpec as P

HEAD_DIM = 64
SYMBOLS = 24
SEQ = 160
PARTS = (2, 2, 2)
RING = 8
BLOCK = 384
TAIL = 16
EPS = 1e-05
SCALE = HEAD_DIM**-0.5
VMEM_LIMIT = 7 * 1024 * 1024

root_half = 0.7071067811865476
root_two_pi = 0.3989422804014327
BF = jnp.bfloat16
F32 = jnp.float32


def swap(value):
    return lax.ppermute(value, "tensor", [(0, 1), (1, 0)])


def dot(a, b):
    return jnp.dot(a, b, preferred_element_type=F32)


def dot_rows(a, b):
    return lax.dot_general(a, b, (((1,), (1,)), ((), ())), preferred_element_type=F32)


def dot_cols(a, b):
    return lax.dot_general(a, b, (((0,), (0,)), ((), ())), preferred_element_type=F32)


def in_order(core, own, other):
    first = core == 0
    return jnp.concatenate(
        [jnp.where(first, own, other), jnp.where(first, other, own)], axis=1
    )


def own_part(core, value):
    half = value.shape[1] // 2
    return jnp.where(core == 0, value[:, :half], value[:, half:])


def normalise(rows):
    centred = rows - jnp.mean(rows, axis=-1, keepdims=True)
    inv_root = lax.rsqrt(jnp.mean(centred * centred, axis=-1, keepdims=True) + EPS)
    return centred * inv_root, inv_root


def norm_back(grads, normal, inv_root, gain):
    scaled = grads * gain
    inner = (
        scaled
        - jnp.mean(scaled, axis=-1, keepdims=True)
        - normal * jnp.mean(scaled * normal, axis=-1, keepdims=True)
    )
    return inner * inv_root


def pair_spans(width):
    return [slice(at, at + 2 * HEAD_DIM) for at in range(0, width, 2 * HEAD_DIM)]


def left_head():
    return lax.broadcasted_iota(jnp.int32, (1, 2 * HEAD_DIM), 1) < HEAD_DIM


def pair_scores(first, second):
    left = left_head().astype(BF)
    both = jnp.concatenate([first * left, first * (1 - left)], axis=0)
    return dot_rows(both, second).reshape(2, SEQ, SEQ)


def pair_product(matrices, block):
    found = dot(matrices.reshape(2 * SEQ, SEQ), block)
    return jnp.where(left_head(), found[:SEQ], found[SEQ:]).astype(BF)


def pair_turned(matrices):
    return jnp.concatenate([matrices[0].T, matrices[1].T], axis=0)


def attn_forward_kernel(start, count, chain, marks, own, other, joint, output, *refs):
    tag = marks[3 + start + chain]
    core = marks[1]
    a, b = own[...], other[...]
    rows = in_order(core, a, b)
    q, k, v = [dot(rows, joint[tag, j]).astype(BF) for j in range(3)]
    key_live = lax.broadcasted_iota(jnp.int32, (1, SEQ, 1), 1) < marks[3 + count + start + chain]
    spans = pair_spans(q.shape[1])
    scores = [pair_scores(k[:, s], q[:, s] * jnp.asarray(SCALE, BF)) for s in spans]
    probs = []
    for found in scores:
        found = jnp.where(key_live, found, -1000000000.0)
        shifted = jnp.exp(found - jnp.max(found, axis=1, keepdims=True))
        probs.append((shifted * (1.0 / jnp.sum(shifted, axis=1, keepdims=True))).astype(BF))
    mixed = jnp.concatenate(
        [pair_product(pair_turned(p), v[:, s]) for p, s in zip(probs, spans)], axis=1
    )
    refs[0][...] = rows
    refs[1][...] = dot(mixed, output[tag]).astype(BF)
    refs[2][...] = jnp.concatenate([q, k, v], axis=1)
    for at, found in enumerate(probs):
        refs[3][0, 2 * at : 2 * at + 2] = found
    refs[4][...] = mixed


def feed_forward_kernel(start, chain, marks, rows, part, other, gains, shifts, up, bias, down, *outs):
    tag = marks[3 + start + chain]
    total = rows[...].astype(F32) + (part[...].astype(F32) + other[...].astype(F32))
    normal, inv_root = normalise(total)
    low = (normal * gains[0:1] + shifts[0:1]).astype(BF)
    pre = dot(low, up[tag]) + jnp.where(tag == 0, bias[0:1], bias[1:2]).astype(F32)
    cdf = 0.5 * (1.0 + lax.erf(pre * root_half))
    hidden = (pre * cdf).astype(BF)
    outs[0][...] = dot(hidden, down[tag]).astype(BF)
    outs[1][...] = normal
    outs[2][...] = inv_root
    outs[3][...] = low
    outs[4][...] = hidden
    outs[5][...] = (cdf + pre * jnp.exp(-0.5 * pre * pre) * root_two_pi).astype(BF)


def second_norm(normal, part, other, gains, shifts):
    first = normal[...] * gains[0:1] + shifts[0:1]
    return normalise(first + (part[...].astype(F32) + other[...].astype(F32)))


def last_norm_kernel(chain, marks, normal, part, other, gains, shifts, out):
    second, _ = second_norm(normal, part, other, gains, shifts)
    out[...] = own_part(marks[1], (second * gains[1:2] + shifts[1:2]).astype(BF))


def add_sums(grads, normal, sums):
    sums[0] += jnp.sum(grads * normal, axis=0, keepdims=True)
    sums[1] += jnp.sum(grads, axis=0, keepdims=True)


def feed_back_kernel(
    start, chain, marks, normal, part, other, gains, shifts, own, partner, slope, up, down, *outs
):
    tag = marks[3 + start + chain]
    core = marks[1]
    a, b = own[...], partner[...]
    grads = in_order(core, a, b).astype(F32)
    second, inv_root = second_norm(normal, part, other, gains, shifts)
    back = norm_back(grads, second, inv_root, gains[1:2])
    low = back.astype(BF)
    d_pre = (dot(low, down[tag]) * slope[...].astype(F32)).astype(BF)
    outs[0][...] = back
    outs[1][...] = dot(d_pre, up[tag]).astype(BF)
    outs[2][...] = low
    outs[3][...] = d_pre
    outs[4][...] = own_part(core, (second * gains[1:2] + shifts[1:2]).astype(BF))
    add_sums(grads, second, outs[5])
    outs[6][tag] += jnp.sum(d_pre.astype(F32), axis=0, keepdims=True)


def attn_back_kernel(
    start, chain, marks, back, part, other, normal, inv_root, gains, joined, probs, joint, output, *outs
):
    tag = marks[3 + start + chain]
    core = marks[1]
    grads = back[...] + (part[...].astype(F32) + other[...].astype(F32))
    back_one = norm_back(grads, normal[...], inv_root[...], gains[0:1])
    low = back_one.astype(BF)
    d_mixed = dot_rows(low, output[tag]).astype(BF)
    width = d_mixed.shape[1]
    q, k, v = [joined[:, j * width : (j + 1) * width] for j in range(3)]
    spans = pair_spans(width)
    d_probs = [pair_scores(v[:, s], d_mixed[:, s]) for s in spans]
    held = [probs[0, 2 * at : 2 * at + 2] for at in range(len(spans))]
    d_scores = []
    for found, kept in zip(d_probs, held):
        wide = kept.astype(F32)
        inner = jnp.sum(wide * found, axis=1, keepdims=True)
        d_scores.append((wide * (found - inner)).astype(BF))
    scale = jnp.asarray(SCALE, BF)
    d_k = [pair_product(d, q[:, s]) * scale for d, s in zip(d_scores, spans)]
    d_v = [pair_product(h, d_mixed[:, s]) for h, s in zip(held, spans)]
    d_q = [pair_product(pair_turned(d), k[:, s]) * scale for d, s in zip(d_scores, spans)]
    pieces = [d_q, d_k, d_v]
    blocks = [jnp.concatenate(p, axis=1) for p in pieces]
    d_rows = sum(dot_rows(blocks[j], joint[tag, j]) for j in range(3)).astype(BF)
    outs[0][...] = own_part(core, back_one) + own_part(core, d_rows).astype(F32)
    outs[1][...] = own_part(1 - core, d_rows)
    outs[2][...] = low
    outs[3][...] = jnp.concatenate(blocks, axis=1)
    add_sums(grads, normal[...], outs[4])


def behind(kernel, taken, ignored):
    def call(marks, *refs):
        kernel(marks, *refs[:taken], *refs[taken + ignored :])

    return call


ANY = pl.BlockSpec(memory_space=pl.ANY)
HBM = pl.BlockSpec(memory_space=pltpu.HBM)
TOKEN = jax.ShapeDtypeStruct((8, 128), F32)
TOKEN_BLOCK = pl.BlockSpec((8, 128), lambda *_: (0, 0))


def sign_off(token):
    token[...] = jnp.zeros_like(token)


class Order:
    def __init__(self):
        self.tokens = ()

    def run(self, call, *args):
        *results, token = call(*args, self.tokens)
        self.tokens = (token,)
        return results

    def wait(self, value):
        self.tokens = tuple(lax.optimization_barrier((*self.tokens, value))[:-1])

    def after(self, value):
        return lax.optimization_barrier((value, *self.tokens))[0]


VMEM = pl.BlockSpec(memory_space=pltpu.VMEM)
SMEM = pl.BlockSpec(memory_space=pltpu.SMEM)


def chain_view(ref, kind, at):
    if kind == "rows":
        return ref.at[at * SEQ : (at + 1) * SEQ]
    return ref.at[at : at + 1] if kind == "chain" else ref


def prepare_kernel(chains, count, places, *refs):
    sources, marks, held = refs[:count], refs[count], refs[count + 1 : 2 * count - 1]
    tags, live, sems = refs[2 * count - 1 :]
    copies = [
        pltpu.make_async_copy(source, target, sems.at[at])
        for at, (source, target) in enumerate(zip(sources, (tags, live) + held))
    ]
    for copy in copies:
        copy.start()
    for at in range(3):
        marks[at] = places[at]
    for copy in copies[:2]:
        copy.wait()
    token = lax.broadcasted_iota(jnp.int32, live.shape, 1)
    for chain in range(chains):
        marks[3 + chain] = jnp.where(tags[chain] > 0, 1, 0)
        inside = (token >= chain * SEQ) & (token < (chain + 1) * SEQ)
        marks[3 + chains + chain] = jnp.sum(jnp.where(inside, live[...], 0))
    for copy in copies[2:]:
        copy.wait()


def prepare(places, tags, live, arrays):
    chains = tags.shape[0]
    sources = [tags, live, *arrays]
    count = len(sources)
    return pl.pallas_call(
        functools.partial(prepare_kernel, chains, count),
        in_specs=[SMEM] + [HBM] * count,
        out_specs=[SMEM] + [VMEM] * len(arrays),
        out_shape=[jax.ShapeDtypeStruct((3 + 2 * chains,), jnp.int32)]
        + [jax.ShapeDtypeStruct(a.shape, a.dtype) for a in arrays],
        scratch_shapes=[
            pltpu.SMEM(tags.shape, jnp.int32),
            pltpu.VMEM(live.shape, jnp.int32),
            pltpu.SemaphoreType.DMA((count,)),
        ],
        compiler_params=pltpu.CompilerParams(vmem_limit_bytes=1024 * 1024),
        name="prepare",
    )(places, *[pltpu.with_memory_space_constraint(a, pltpu.HBM) for a in sources])


def turn(active, marks, arrays, held, after):
    count = len(arrays)
    skipped = count + len(held) + len(after)

    def call(marks, *refs):
        sign_off(refs[-1])

        @pl.when(marks[0] == active)
        def _():
            for source, target in zip(refs[:count], refs[skipped:]):
                for at in range(source.shape[0]):
                    target[at] = source[at].T

    return pl.pallas_call(
        call,
        in_specs=[SMEM] + [VMEM] * (count + len(held)) + [ANY] * len(after),
        out_specs=[VMEM] * (count + 1),
        out_shape=[jax.ShapeDtypeStruct((a.shape[0], a.shape[2], a.shape[1]), BF) for a in arrays]
        + [TOKEN],
        input_output_aliases={1 + count + at: at for at in range(len(held))},
        compiler_params=pltpu.CompilerParams(vmem_limit_bytes=VMEM_LIMIT),
        cost_estimate=pl.CostEstimate(flops=10**10, bytes_accessed=10**7, transcendentals=0),
        name="turn",
    )(marks, *arrays, *held, *after)


def run_chains(kernel, name, active, marks, chains, ins, outs, after):
    shapes, held, aliases = [], [], {}
    for trailing, dtype, kind, array in outs:
        lead = {"rows": (chains * SEQ,), "chain": (chains,), "whole": ()}[kind]
        if array is not None:
            aliases[1 + len(ins) + len(held)] = len(shapes)
            held.append(array)
        shapes.append(jax.ShapeDtypeStruct(lead + trailing, dtype))
    kinds = [(kind, first) for _, kind, first in ins] + [(kind, 0) for _, _, kind, _ in outs]
    skipped = len(ins) + len(held) + len(after)

    def call(marks, *refs):
        *refs, token = refs[: len(ins)] + refs[skipped:]
        sign_off(token)

        @pl.when(marks[0] == active)
        def _():
            for chain in range(chains):
                views = [chain_view(r, kind, first + chain) for r, (kind, first) in zip(refs, kinds)]
                kernel(chain, marks, *views)

    return pl.pallas_call(
        call,
        in_specs=[SMEM] + [VMEM] * (len(ins) + len(held)) + [ANY] * len(after),
        out_specs=[VMEM] * (len(outs) + 1),
        out_shape=shapes + [TOKEN],
        input_output_aliases=aliases,
        compiler_params=pltpu.CompilerParams(vmem_limit_bytes=VMEM_LIMIT),
        cost_estimate=pl.CostEstimate(flops=10**10, bytes_accessed=10**7, transcendentals=0),
        name=name,
    )(marks, *[a for a, _, _ in ins], *held, *after)


def ring_spot(marks, step, way):
    return lax.rem(marks[2] + 2 * RING + way * step, RING)


def span(at):
    return pl.ds(pl.multiple_of(at * BLOCK, BLOCK), BLOCK)


def cut(ref, at):
    return ref[:, span(at)]


def set_rows(marks, block, which):
    pieces = []
    for chain in range(block.shape[0] // SEQ):
        piece = block[chain * SEQ : (chain + 1) * SEQ]
        pieces.append(jnp.where(marks[3 + chain] == which, piece, jnp.zeros_like(piece)))
    return jnp.concatenate(pieces, axis=0)


def all_rows(refs, at):
    return jnp.concatenate([cut(ref, at) for ref in refs], axis=0)


def feed_shard(marks, which, hidden, d_down, low, d_pre):
    return (
        dot_cols(set_rows(marks, hidden, which), d_down).astype(BF),
        dot_cols(set_rows(marks, low, which), d_pre).astype(BF),
    )


def feed_weights_kernel(step, parts, marks, *refs):
    hidden, d_down, low, d_pre = [refs[n * parts : (n + 1) * parts] for n in range(4)]
    out, token = refs[4 * parts :]
    sign_off(token)
    for which, way in ((0, -1), (1, 1)):
        spot = ring_spot(marks, step, way)
        far, near = lax.div(spot, 2), lax.rem(spot, 2)
        out[which, :BLOCK], out[which, BLOCK:] = feed_shard(
            marks,
            which,
            all_rows(hidden, far),
            all_rows(d_down, near),
            all_rows(low, near),
            all_rows(d_pre, far),
        )


def two_halves(value):
    high = value.astype(BF).astype(F32)
    return jnp.concatenate([high, value - high], axis=0).astype(BF)


def one_whole(rows):
    rows = rows.astype(F32)
    return rows[: TAIL // 2] + rows[TAIL // 2 :]


def count_rows(live, predicted, targets):
    symbols = lax.broadcasted_iota(jnp.int32, (128, live.shape[1]), 0)
    hits = (targets[...] == symbols) & (live[...] > 0)
    right = hits & (predicted[...] == targets[...])
    ones = jnp.ones((8, live.shape[1]), BF)
    found = [dot_rows(ones, h.astype(F32).astype(BF)) for h in (hits, right)]
    return jnp.concatenate(found + [jnp.zeros_like(found[0])], axis=1)[0:1]


def attn_weights_kernel(step, parts, marks, *refs):
    rows, d_joined, mixed, d_attn = [refs[n * parts : (n + 1) * parts] for n in range(4)]
    bias, *sums, live, predicted, targets, out, token = refs[4 * parts :]
    sign_off(token)
    for which, way in ((0, -1), (1, 1)):
        spot = ring_spot(marks, step, way)
        far, near = lax.div(spot, 2), lax.rem(spot, 2)

        @pl.when(far < 3)
        def _():
            out[which, :BLOCK] = dot_cols(
                set_rows(marks, all_rows(rows, near), which), all_rows(d_joined, far)
            ).astype(BF)

        @pl.when(far == 3)
        def _():
            out[which, :BLOCK] = dot_cols(
                set_rows(marks, all_rows(mixed, 0), which), all_rows(d_attn, near)
            ).astype(BF)

        early = far < 2
        small = jnp.where(
            early,
            bias[which, :, span(jnp.where(early, spot, 0))],
            sums[which][jnp.where(early, 0, far - 2), :, span(near)],
        )
        place = lax.broadcasted_iota(jnp.int32, (TAIL // 2, BLOCK), 0)
        small = jnp.where(place == 0, small, 0.0)
        out[which, BLOCK:] = two_halves(small)
        if which == 0:

            @pl.when(spot == 0)
            def _():
                counts = count_rows(live, predicted, targets)
                out[which, BLOCK:] = two_halves(jnp.where(place == 1, counts, small))


def run_weights(kernel, name, marks, step, lists, rest, rows_out, cost, after):
    ins = [a for arrays in lists for a in arrays] + list(rest)
    return pl.pallas_call(
        behind(functools.partial(kernel, step + 1, len(lists[0])), len(ins), len(after)),
        in_specs=[SMEM] + [VMEM] * len(ins) + [ANY] * len(after),
        out_specs=[VMEM, VMEM],
        out_shape=[jax.ShapeDtypeStruct((2, rows_out, BLOCK), BF), TOKEN],
        compiler_params=pltpu.CompilerParams(vmem_limit_bytes=VMEM_LIMIT),
        cost_estimate=pl.CostEstimate(flops=cost, bytes_accessed=10**6, transcendentals=0),
        name=name,
    )(marks, *ins, *after)


def add_kernel(tail, ahead, back, local, out_ahead, out_back, token):
    sign_off(token)
    for which, (ref, out) in enumerate(((ahead, out_ahead), (back, out_back))):
        total = ref[...].astype(F32) + local[which].astype(F32)
        out[...] = total.astype(BF)
        if tail:
            out[tail:] = two_halves(one_whole(total[tail:]))


def add_step(pair, local, after):
    shape = local.shape[1:]
    tail = BLOCK if shape[0] == BLOCK + TAIL else 0

    def call(*refs):
        add_kernel(tail, *refs[:3], *refs[3 + len(after) :])

    return pl.pallas_call(
        call,
        in_specs=[VMEM] * 3 + [ANY] * len(after),
        out_specs=[VMEM] * 3,
        out_shape=[jax.ShapeDtypeStruct(shape, BF)] * 2 + [TOKEN],
        compiler_params=pltpu.CompilerParams(vmem_limit_bytes=VMEM_LIMIT),
        cost_estimate=pl.CostEstimate(flops=3*10**9, bytes_accessed=10**6, transcendentals=0),
        name="ring_add",
    )(*pair, local, *after)


def feed_place_kernel(step, marks, ahead, back, outs, wide, sems):
    down, up = outs
    copies = []
    for which, (ref, way) in enumerate(((ahead, -1), (back, 1))):
        spot = ring_spot(marks, step, way)
        far, near = lax.div(spot, 2), lax.rem(spot, 2)
        wide[which] = ref[...].astype(F32)
        copies += [
            pltpu.make_async_copy(
                wide.at[which, :BLOCK], down.at[which, span(far), span(near)], sems.at[2 * which]
            ),
            pltpu.make_async_copy(
                wide.at[which, BLOCK:], up.at[which, span(near), span(far)], sems.at[2 * which + 1]
            ),
        ]
        for copy in copies[-2:]:
            copy.start()
    for copy in copies:
        copy.wait()


def attn_place_kernel(step, marks, ahead, back, outs, wide, sems):
    joint, output, small = outs
    copies = []
    for which, (ref, way) in enumerate(((ahead, -1), (back, 1))):
        spot = ring_spot(marks, step, way)
        far, near = lax.div(spot, 2), lax.rem(spot, 2)
        wide[which] = ref[...].astype(F32)
        wide[which, BLOCK : BLOCK + TAIL // 2] = one_whole(ref[BLOCK:])
        copy = pltpu.make_async_copy(
            wide.at[which, BLOCK : BLOCK + TAIL // 2], small.at[which, spot], sems.at[2 + which]
        )
        copy.start()
        copies.append(copy)

        @pl.when(far < 3)
        def _():
            copy = pltpu.make_async_copy(
                wide.at[which, :BLOCK], joint.at[which, far, span(near)], sems.at[which]
            )
            copy.start()
            copy.wait()

        @pl.when(far == 3)
        def _():
            copy = pltpu.make_async_copy(
                wide.at[which, :BLOCK], output.at[which, :, span(near)], sems.at[which]
            )
            copy.start()
            copy.wait()

    for copy in copies:
        copy.wait()


def place_step(kernel, name, marks, step, pair, held, after):
    shape = pair[0].shape
    block = pl.BlockSpec(shape, lambda i, *_: (0, 0))

    count = len(held)

    def call(marks, ahead, back, *refs):
        refs = refs[count + len(after) :]
        sign_off(refs[count])
        kernel(step, marks, ahead, back, refs[:count], *refs[count + 1 :])

    return pl.pallas_call(
        call,
        grid_spec=pltpu.PrefetchScalarGridSpec(
            num_scalar_prefetch=1,
            grid=(1,),
            in_specs=[block, block] + [HBM] * count + [ANY] * len(after),
            out_specs=[HBM] * count + [TOKEN_BLOCK],
            scratch_shapes=[pltpu.VMEM((2,) + shape, F32), pltpu.SemaphoreType.DMA((4,))],
        ),
        out_shape=[jax.ShapeDtypeStruct(h.shape, h.dtype) for h in held] + [TOKEN],
        input_output_aliases={3 + i: i for i in range(count)},
        compiler_params=pltpu.CompilerParams(vmem_limit_bytes=VMEM_LIMIT),
        cost_estimate=pl.CostEstimate(
            flops=10**10, bytes_accessed=10**6, transcendentals=0
        ),
        name=name,
    )(marks, *pair, *held, *after)


def unwritten(*shapes):
    return pl.pallas_call(
        lambda *refs: None,
        out_specs=[HBM] * len(shapes),
        out_shape=[jax.ShapeDtypeStruct(s, F32) for s in shapes],
        compiler_params=pltpu.CompilerParams(vmem_limit_bytes=1024 * 1024),
        name="unwritten",
    )()


class Ring:
    def __init__(self):
        self.count = lax.axis_size("dp")
        assert self.count % RING == 0
        order = list(range(0, RING, 2)) + list(range(1, RING, 2))[::-1]
        rank = lax.rem(lax.axis_index("dp"), RING)
        self.place = jnp.zeros((), jnp.int32)
        for at, member in enumerate(order):
            self.place = jnp.where(rank == member, at, self.place)
        self.ahead = [
            (base + order[i], base + order[(i + 1) % RING])
            for base in range(0, self.count, RING)
            for i in range(RING)
        ]
        self.back = [(b, a) for a, b in self.ahead]

    def send(self, pair):
        return lax.ppermute(pair[0], "dp", self.ahead), lax.ppermute(pair[1], "dp", self.back)

    def across(self, pair):
        result = []
        for value in pair:
            total = value.astype(F32)
            moving = value
            for _ in range(self.count // RING - 1):
                pairs = [(i, (i + RING) % self.count) for i in range(self.count)]
                moving = lax.ppermute(moving, "dp", pairs)
                total = total + moving.astype(F32)
            low = total.astype(BF)
            if total.shape[0] == BLOCK + TAIL and self.count > RING:
                tail = two_halves(one_whole(total[BLOCK:]))
                low = jnp.concatenate([low[:BLOCK], tail], axis=0)
            result.append(low)
        return result


def part_sizes(chains):
    bounds = [chains * sum(PARTS[:p]) // sum(PARTS) for p in range(len(PARTS) + 1)]
    return [high - low for low, high in zip(bounds, bounds[1:])], bounds[:-1]


def shards(
    chain_inputs,
    cotangent,
    chain_tags,
    pad_mask,
    predicted,
    target_ids,
    joint_proj,
    output_proj,
    up_proj,
    up_bias,
    down_proj,
    norm_gain,
    norm_shift,
):
    section = lax.axis_index("section")
    core = lax.axis_index("tensor")
    tokens, half = chain_inputs.shape
    width = 2 * half
    all_chains = tokens // SEQ
    sizes, starts = part_sizes(all_chains)
    parts = range(len(sizes))
    ring = Ring()
    small = [ids.reshape(1, tokens) for ids in (pad_mask, predicted, target_ids)]
    joint = joint_proj[0].transpose(0, 2, 1, 3)
    output, up, bias, down = output_proj[0], up_proj[0], up_bias[0], down_proj[0]
    places = jnp.stack([section, core, ring.place]).astype(jnp.int32)
    marks, joint, output, own_rows = prepare(
        places, chain_tags, small[0], [joint, output, chain_inputs]
    )
    gains, shifts = norm_gain[0], norm_shift[0]
    units = up.shape[2]
    local = output.shape[1]
    heads = local // HEAD_DIM
    cot_other = swap(cotangent)
    rows_other = swap(chain_inputs)

    order = Order()

    kept = [{} for _ in parts]
    feed = [{} for _ in parts]
    attn = [{} for _ in parts]
    sent = [{} for _ in parts]
    sums = dict(
        feed=jnp.zeros((2, 1, width), F32),
        attn=jnp.zeros((2, 1, width), F32),
        bias=jnp.zeros((2, 1, units), F32),
    )

    def run(kernel, name, active, p, ins, outs, held, totals):
        outs = [(shape, dtype, kind, held.get(key)) for key, shape, dtype, kind in outs] + [
            (sums[key].shape, F32, "whole", sums[key]) for key in totals
        ]
        return order.run(run_chains, kernel, name, active, marks, sizes[p], ins, outs)

    def attn_forward(active, p, own, other, first):
        ins = [(own, "rows", first), (other, "rows", first)]
        ins += [(joint, "whole", 0), (output, "whole", 0)]
        outs = [
            ("rows", (width,), BF, "rows"),
            ("part", (width,), BF, "rows"),
            ("joined", (3 * local,), BF, "rows"),
            ("probs", (heads, SEQ, SEQ), BF, "chain"),
            ("mixed", (local,), BF, "rows"),
        ]
        kernel = functools.partial(attn_forward_kernel, starts[p], all_chains)
        found = run(kernel, "attn_forward", active, p, ins, outs, kept[p], [])
        kept[p].update(zip([o[0] for o in outs], found))
        kept[p]["part_other"] = swap(kept[p]["part"])

    def feed_forward(active, p):
        ins = [(kept[p][n], "rows", 0) for n in ("rows", "part", "part_other")]
        ins += [(a, "whole", 0) for a in (gains, shifts, up, bias, down)]
        outs = [
            ("down", (width,), BF, "rows"),
            ("normal", (width,), F32, "rows"),
            ("inv_root", (1,), F32, "rows"),
            ("low", (width,), BF, "rows"),
            ("hidden", (units,), BF, "rows"),
            ("slope", (units,), BF, "rows"),
        ]
        kernel = functools.partial(feed_forward_kernel, starts[p])
        found = run(kernel, "feed_forward", active, p, ins, outs, kept[p], [])
        kept[p].update(zip([o[0] for o in outs], found))
        kept[p]["down_other"] = swap(kept[p]["down"])

    def feed_back(active, p, own, other, first):
        ins = [(kept[p][n], "rows", 0) for n in ("normal", "down", "down_other")]
        ins += [(gains, "whole", 0), (shifts, "whole", 0)]
        ins += [(own, "rows", first), (other, "rows", first)]
        ins += [(kept[p]["slope"], "rows", 0)]
        ins += [(turned["up"], "whole", 0), (turned["down"], "whole", 0)]
        outs = [
            ("back", (width,), F32, "rows"),
            ("part", (width,), BF, "rows"),
            ("d_down", (width,), BF, "rows"),
            ("d_pre", (units,), BF, "rows"),
            ("outputs", (half,), BF, "rows"),
        ]
        kernel = functools.partial(feed_back_kernel, starts[p])
        *found, sums["feed"], sums["bias"] = run(
            kernel, "feed_back", active, p, ins, outs, feed[p], ["feed", "bias"]
        )
        feed[p].update(zip([o[0] for o in outs], found))
        feed[p]["part_other"] = swap(feed[p]["part"])

    def attn_back(active, p):
        ins = [(feed[p][n], "rows", 0) for n in ("back", "part", "part_other")]
        ins += [(kept[p]["normal"], "rows", 0), (kept[p]["inv_root"], "rows", 0)]
        ins += [(gains, "whole", 0), (kept[p]["joined"], "rows", 0), (kept[p]["probs"], "chain", 0)]
        ins += [(joint, "whole", 0), (output, "whole", 0)]
        outs = [
            ("mine", (half,), F32, "rows"),
            ("theirs", (half,), BF, "rows"),
            ("d_attn", (width,), BF, "rows"),
            ("d_joined", (3 * local,), BF, "rows"),
        ]
        kernel = functools.partial(attn_back_kernel, starts[p])
        *found, sums["attn"] = run(kernel, "attn_back", active, p, ins, outs, attn[p], ["attn"])
        attn[p].update(zip([o[0] for o in outs], found))

    def input_gradient(p, theirs):
        return attn[p]["mine"] + swap(theirs).astype(F32)

    def across(value):
        return lax.ppermute(value, "section", [(0, 1), (1, 0)])

    turned = {}

    def turn_weights(active):
        held = [turned[n] for n in ("up", "down") if n in turned]
        turned["up"], turned["down"] = order.run(turn, active, marks, [up, down], held)

    def attn_early(p):
        attn_forward(0, p, own_rows, rows_other, starts[p])

    def feed_early(p):
        feed_forward(0, p)

    def hand_on(p):
        ins = [(kept[p][n], "rows", 0) for n in ("normal", "down", "down_other")]
        ins += [(gains, "whole", 0), (shifts, "whole", 0)]
        outs = [("moved", (half,), BF, "rows")]
        found = run(last_norm_kernel, "last_norm", 0, p, ins, outs, {}, [])
        sent[p]["on"] = across(found[0])

    def receive(p):
        moved = order.after(sent[p]["on"])
        sent[p]["on"] = (moved, swap(moved))

    def attn_late(p):
        attn_forward(1, p, *sent[p]["on"], 0)

    def feed_late(p):
        feed_forward(1, p)

    def feed_first(p):
        feed_back(1, p, cotangent, cot_other, starts[p])

    def attn_first(p):
        attn_back(1, p)
        sent[p]["back"] = across(input_gradient(p, attn[p]["theirs"]).astype(BF))

    def receive_back(p):
        moved = order.after(sent[p]["back"])
        sent[p]["back"] = (moved, swap(moved))

    def feed_last(p):
        feed_back(0, p, *sent[p]["back"], 0)

    def attn_last(p):
        attn_back(0, p)

    for step, p in (
        (attn_early, 0),
        (attn_early, 1),
        (feed_early, 0),
        (turn_weights, 1),
        (hand_on, 0),
        (feed_early, 1),
        (attn_early, 2),
        (receive, 0),
        (attn_late, 0),
        (hand_on, 1),
        (feed_late, 0),
        (feed_early, 2),
        (feed_first, 0),
        (hand_on, 2),
        (receive, 1),
        (attn_first, 0),
        (attn_late, 1),
        (receive, 2),
        (turn_weights, 0),
        (feed_late, 1),
        (attn_late, 2),
        (feed_first, 1),
        (feed_late, 2),
        (receive_back, 0),
        (attn_first, 1),
        (feed_last, 0),
        (feed_first, 2),
        (receive_back, 1),
        (attn_first, 2),
        (feed_last, 1),
        (receive_back, 2),
        (feed_last, 2),
    ):
        step(p)
    feed_lists = [
        [kept[p]["hidden"] for p in parts],
        [feed[p]["d_down"] for p in parts],
        [kept[p]["low"] for p in parts],
        [feed[p]["d_pre"] for p in parts],
    ]

    def feed_weights(step, cost=3 * 10**9):
        return order.run(
            run_weights,
            feed_weights_kernel,
            "feed_weights",
            marks,
            step,
            feed_lists,
            [],
            2 * BLOCK,
            cost,
        )[0]

    def add_local(pair, local):
        return order.run(add_step, pair, local)

    shard = feed_weights(0)
    feed_pair = ring.send((shard[0], shard[1]))
    shard = feed_weights(1)
    for p in parts:
        attn_last(p)
    feed_pair = ring.send(add_local(feed_pair, shard))
    attn_lists = [
        [kept[p]["rows"] for p in parts],
        [attn[p]["d_joined"] for p in parts],
        [kept[p]["mixed"] for p in parts],
        [attn[p]["d_attn"] for p in parts],
    ]

    small = [sums["bias"], sums["attn"], sums["feed"], *small]

    def attn_weights(step, cost=3 * 10**9):
        return order.run(
            run_weights,
            attn_weights_kernel,
            "attn_weights",
            marks,
            step,
            attn_lists,
            small,
            BLOCK + TAIL,
            cost,
        )[0]

    shard = attn_weights(0, 10**9)
    attn_pair = ring.send((shard[0], shard[1]))
    attn_local = attn_weights(1, 10**9)
    feed_local = feed_weights(2, 10**9)
    streams = [
        dict(
            pair=attn_pair,
            local=attn_local,
            weights=attn_weights,
            sent=1,
            kernel=attn_place_kernel,
            name="attn_place",
            held=unwritten((2, 3, width, local), (2, local, width), (2, RING, 8, BLOCK)),
        ),
        dict(
            pair=feed_pair,
            local=feed_local,
            weights=feed_weights,
            sent=2,
            kernel=feed_place_kernel,
            name="feed_place",
            held=unwritten((2, units, width), (2, width, units)),
        ),
    ]

    def advance(stream):
        sent = stream["sent"]
        *pair, token = lax.optimization_barrier((*stream["pair"], *order.tokens))
        order.tokens = (token,)
        if sent < RING:
            pair = add_local(pair, stream["local"])
            if sent == RING - 1:
                pair = ring.across(pair)
        stream["pair"] = ring.send(pair) if sent < 2 * RING - 2 else None
        if sent < RING - 1:
            stream["local"] = stream["weights"](sent + 1)
        else:
            stream["held"] = order.run(
                place_step,
                stream["kernel"],
                stream["name"],
                marks,
                sent - RING + 1,
                pair,
                stream["held"],
            )
        stream["sent"] += 1

    attn_stream, feed_stream = streams
    input_grads = []
    while attn_stream["pair"] is not None or feed_stream["pair"] is not None:
        if attn_stream["sent"] == 2 * RING - 2:
            input_grads = [input_gradient(p, order.after(attn[p]["theirs"])) for p in parts]
        if feed_stream["pair"] is not None:
            advance(feed_stream)
        if attn_stream["pair"] is not None:
            advance(attn_stream)
    joint_out, output_out, small_out = attn_stream["held"]
    down_out, up_out = feed_stream["held"]

    def whole(pieces):
        return jnp.concatenate(pieces, axis=0)

    input_grads = whole(input_grads)
    rows = small_out[:, :, 0]
    bias_grad = rows[:, :4].reshape(2, units)
    norm_sums = rows[:, 4:].reshape(2, 2, width)
    counts = small_out[0, 0, 1].reshape(3, 128)[:2, :SYMBOLS]
    return (
        whole([feed[p]["outputs"] for p in parts])[None],
        input_grads[None],
        joint_out.transpose(0, 2, 1, 3)[None],
        output_out[None],
        up_out[None],
        bias_grad[None],
        down_out[None],
        norm_sums[:, 0][None],
        norm_sums[:, 1][None],
        counts.astype(jnp.int32),
    )


def solution(mesh):
    return jax.shard_map(
        shards,
        mesh=mesh,
        in_specs=(
            P("dp", "tensor"),
            P("dp", "tensor"),
            P("dp"),
            P("dp"),
            P("dp"),
            P("dp"),
            P("section", None, None, None, "tensor"),
            P("section", None, "tensor", None),
            P("section", None, None, "tensor"),
            P("section", None, "tensor"),
            P("section", None, "tensor", None),
            P("section", None, None),
            P("section", None, None),
        ),
        out_specs=(
            P("section", "dp", "tensor"),
            P("section", "dp", "tensor"),
            P("section", None, None, None, "tensor"),
            P("section", None, "tensor", None),
            P("section", None, None, "tensor"),
            P("section", None, "tensor"),
            P("section", None, "tensor", None),
            P("section", None, None),
            P("section", None, None),
            P(),
        ),
        check_vma=False,
    )
```

profile of v0, /device:TPU:0, one launch (start us, length us, event | category | flops | bytes accessed | tf_op | source)
XLA Modules:
  0.0 395.1 jit_solution(110178570338971850)
XLA Ops:
  1.2 3.7 prepare.1
  18.2 3.4 feed_forward.7
  33.0 3.6 feed_forward.9
  49.9 4.3 %collective-permute-start.14 = (bf16[320,384]{1,0:T(8,128)(2,1)S(1)}, bf16[320,384]{1,0:T(8,128)(2,1)S(1)}, u32[]{:S(2)}, u32[]{:S(2)}) collective-permute-start(bf16[320,384]{1,0:T(8,128)(2,1)S(1)} %add_convert_fusion.2), channel_id=1, source_target_pairs={{0,16},{16,0},{1,17},{17,1},{2,18},{18,2},{3,19},{19,3},{4,20},{20... | collective-permute-start | bytes 737288 | tf_op jit(solution)/shard_map/ppermute | solution.py:752
  67.3 12.3 %collective-permute-start.25 = (bf16[320,384]{1,0:T(8,128)(2,1)S(1)}, bf16[320,384]{1,0:T(8,128)(2,1)S(1)}, u32[]{:S(2)}, u32[]{:S(2)}) collective-permute-start(bf16[320,384]{1,0:T(8,128)(2,1)S(1)} %add_convert_fusion.1), channel_id=1, source_target_pairs={{0,16},{16,0},{1,17},{17,1},{2,18},{18,2},{3,19},{19,3},{4,20},{20... | collective-permute-start | bytes 737288 | tf_op jit(solution)/shard_map/ppermute | solution.py:752
  80.4 5.7 %collective-permute-done.25.refs_5_ = bf16[320,384]{1,0:T(8,128)(2,1)S(1)} collective-permute-done((bf16[320,384]{1,0:T(8,128)(2,1)S(1)}, bf16[320,384]{1,0:T(8,128)(2,1)S(1)}, u32[]{:S(2)}, u32[]{:S(2)}) %collective-permute-start.25) | collective-permute-done | bytes 245792 | tf_op jit(solution)/shard_map/ppermute | solution.py:752
  88.0 3.8 feed_back.10
  107.6 4.3 %attn_back.9 = (f32[320,384]{1,0:T(8,128)S(1)}, bf16[320,384]{1,0:T(8,128)(2,1)S(1)}, bf16[320,768]{1,0:T(8,128)(2,1)S(1)}, bf16[320,1152]{1,0:T(8,128)(2,1)S(1)...) custom-call(s32[15]{0:T(128)S(1)} %get-tuple-element.412.marks, ...), custom_call_target="tpu_custom_call", output_to_operand_aliasing={{0}: (11, {}), {1}: (12, {}), {2}: (13, {}), {3}: (14, {}),... | custom-call | flops 10000000000 | bytes 10000000 | tf_op jit(solution)/shard_map/attn_back/pallas_call | solution.py:335
  111.9 4.4 %attn_back.10 = (f32[320,384]{1,0:T(8,128)S(1)}, bf16[320,384]{1,0:T(8,128)(2,1)S(1)}, bf16[320,768]{1,0:T(8,128)(2,1)S(1)}, bf16[320,1152]{1,0:T(8,128)(2,1)S(1...) custom-call(s32[15]{0:T(128)S(1)} %get-tuple-element.412.marks, ...), custom_call_target="tpu_custom_call", output_to_operand_aliasing={{0}: (11, {}), {1}: (12, {}), {2}: (13, {}), {3}: (14, {}),... | custom-call | flops 10000000000 | bytes 10000000 | tf_op jit(solution)/shard_map/attn_back/pallas_call | solution.py:335
  116.3 4.2 %attn_back.11 = (f32[320,384]{1,0:T(8,128)S(1)}, bf16[320,384]{1,0:T(8,128)(2,1)S(1)}, bf16[320,768]{1,0:T(8,128)(2,1)S(1)}, bf16[320,1152]{1,0:T(8,128)(2,1)S(1...) custom-call(s32[15]{0:T(128)S(1)} %get-tuple-element.412.marks, ...), custom_call_target="tpu_custom_call", output_to_operand_aliasing={{0}: (11, {}), {1}: (12, {}), {2}: (13, {}), {3}: (14, {}),... | custom-call | flops 10000000000 | bytes 10000000 | tf_op jit(solution)/shard_map/attn_back/pallas_call | solution.py:335
  132.2 5.7 %collective-permute-done.39.refs_0_ = bf16[768,384]{1,0:T(8,128)(2,1)S(1)} collective-permute-done((bf16[768,384]{1,0:T(8,128)(2,1)S(1)}, bf16[768,384]{1,0:T(8,128)(2,1)S(1)}, u32[]{:S(2)}, u32[]{:S(2)}) %collective-permute-start.39) | collective-permute-done | bytes 589856 | tf_op jit(solution)/shard_map/ppermute | solution.py:603
  150.6 6.5 %collective-permute-done.43.refs_0_ = bf16[768,384]{1,0:T(8,128)(2,1)S(1)} collective-permute-done((bf16[768,384]{1,0:T(8,128)(2,1)S(1)}, bf16[768,384]{1,0:T(8,128)(2,1)S(1)}, u32[]{:S(2)}, u32[]{:S(2)}) %collective-permute-start.43) | collective-permute-done | bytes 589856 | tf_op jit(solution)/shard_map/ppermute | solution.py:603
  169.8 6.5 %collective-permute-done.47.refs_0_ = bf16[768,384]{1,0:T(8,128)(2,1)S(1)} collective-permute-done((bf16[768,384]{1,0:T(8,128)(2,1)S(1)}, bf16[768,384]{1,0:T(8,128)(2,1)S(1)}, u32[]{:S(2)}, u32[]{:S(2)}) %collective-permute-start.47) | collective-permute-done | bytes 589856 | tf_op jit(solution)/shard_map/ppermute | solution.py:603
  189.1 6.5 %collective-permute-done.51.refs_0_ = bf16[768,384]{1,0:T(8,128)(2,1)S(1)} collective-permute-done((bf16[768,384]{1,0:T(8,128)(2,1)S(1)}, bf16[768,384]{1,0:T(8,128)(2,1)S(1)}, u32[]{:S(2)}, u32[]{:S(2)}) %collective-permute-start.51) | collective-permute-done | bytes 589856 | tf_op jit(solution)/shard_map/ppermute | solution.py:603
  208.3 6.5 %collective-permute-done.55.refs_0_ = bf16[768,384]{1,0:T(8,128)(2,1)S(1)} collective-permute-done((bf16[768,384]{1,0:T(8,128)(2,1)S(1)}, bf16[768,384]{1,0:T(8,128)(2,1)S(1)}, u32[]{:S(2)}, u32[]{:S(2)}) %collective-permute-start.55) | collective-permute-done | bytes 589856 | tf_op jit(solution)/shard_map/ppermute | solution.py:603
  227.5 6.5 %collective-permute-done.59.refs_0_ = bf16[768,384]{1,0:T(8,128)(2,1)S(1)} collective-permute-done((bf16[768,384]{1,0:T(8,128)(2,1)S(1)}, bf16[768,384]{1,0:T(8,128)(2,1)S(1)}, u32[]{:S(2)}, u32[]{:S(2)}) %collective-permute-start.59) | collective-permute-done | bytes 589856 | tf_op jit(solution)/shard_map/ppermute | solution.py:603
  247.0 6.3 %collective-permute-done.63.ahead = bf16[768,384]{1,0:T(8,128)(2,1)S(1)} collective-permute-done((bf16[768,384]{1,0:T(8,128)(2,1)S(1)}, bf16[768,384]{1,0:T(8,128)(2,1)S(1)}, u32[]{:S(2)}, u32[]{:S(2)}) %collective-permute-start.63) | collective-permute-done | bytes 589856 | tf_op jit(solution)/shard_map/ppermute | solution.py:603
  266.5 6.0 %collective-permute-done.67.ahead = bf16[768,384]{1,0:T(8,128)(2,1)S(1)} collective-permute-done((bf16[768,384]{1,0:T(8,128)(2,1)S(1)}, bf16[768,384]{1,0:T(8,128)(2,1)S(1)}, u32[]{:S(2)}, u32[]{:S(2)}) %collective-permute-start.67) | collective-permute-done | bytes 589856 | tf_op jit(solution)/shard_map/ppermute | solution.py:603
  285.5 6.2 %collective-permute-done.71.ahead = bf16[768,384]{1,0:T(8,128)(2,1)S(1)} collective-permute-done((bf16[768,384]{1,0:T(8,128)(2,1)S(1)}, bf16[768,384]{1,0:T(8,128)(2,1)S(1)}, u32[]{:S(2)}, u32[]{:S(2)}) %collective-permute-start.71) | collective-permute-done | bytes 589856 | tf_op jit(solution)/shard_map/ppermute | solution.py:603
  304.7 6.2 %collective-permute-done.75.ahead = bf16[768,384]{1,0:T(8,128)(2,1)S(1)} collective-permute-done((bf16[768,384]{1,0:T(8,128)(2,1)S(1)}, bf16[768,384]{1,0:T(8,128)(2,1)S(1)}, u32[]{:S(2)}, u32[]{:S(2)}) %collective-permute-start.75) | collective-permute-done | bytes 589856 | tf_op jit(solution)/shard_map/ppermute | solution.py:603
  323.9 6.2 %collective-permute-done.79.ahead = bf16[768,384]{1,0:T(8,128)(2,1)S(1)} collective-permute-done((bf16[768,384]{1,0:T(8,128)(2,1)S(1)}, bf16[768,384]{1,0:T(8,128)(2,1)S(1)}, u32[]{:S(2)}, u32[]{:S(2)}) %collective-permute-start.79) | collective-permute-done | bytes 589856 | tf_op jit(solution)/shard_map/ppermute | solution.py:603
  343.1 6.2 %collective-permute-done.83.ahead = bf16[768,384]{1,0:T(8,128)(2,1)S(1)} collective-permute-done((bf16[768,384]{1,0:T(8,128)(2,1)S(1)}, bf16[768,384]{1,0:T(8,128)(2,1)S(1)}, u32[]{:S(2)}, u32[]{:S(2)}) %collective-permute-start.83) | collective-permute-done | bytes 589856 | tf_op jit(solution)/shard_map/ppermute | solution.py:603
  362.4 6.2 %collective-permute-done.87.ahead = bf16[768,384]{1,0:T(8,128)(2,1)S(1)} collective-permute-done((bf16[768,384]{1,0:T(8,128)(2,1)S(1)}, bf16[768,384]{1,0:T(8,128)(2,1)S(1)}, u32[]{:S(2)}, u32[]{:S(2)}) %collective-permute-start.87) | collective-permute-done | bytes 589856 | tf_op jit(solution)/shard_map/ppermute | solution.py:603
  384.3 4.5 %collective-permute-done.92.ahead = bf16[400,384]{1,0:T(8,128)(2,1)S(1)} collective-permute-done((bf16[400,384]{1,0:T(8,128)(2,1)S(1)}, bf16[400,384]{1,0:T(8,128)(2,1)S(1)}, u32[]{:S(2)}, u32[]{:S(2)}) %collective-permute-start.92) | collective-permute-done | bytes 307232 | tf_op jit(solution)/shard_map/ppermute | solution.py:603
  (398 shorter events, 256.8 us)
Async XLA Ops:
  67.3 18.8 %collective-permute-start.25 = (bf16[320,384]{1,0:T(8,128)(2,1)S(1)}, bf16[320,384]{1,0:T(8,128)(2,1)S(1)}, u32[]{:S(2)}, u32[]{:S(2)}) collective-permute-start(bf16[320,384]{1,0:T(8,128)(2,1)S(1)} %add_convert_fusion.1), channel_id=1, source_target_pairs={{0,16},{16,0},{1,17},{17,1},{2,18},{18,2},{3,19},{19,3},{4,20},{20... | collective-permute-start | bytes 737288 | tf_op jit(solution)/shard_map/ppermute | solution.py:752
  102.2 19.1 %collective-permute-start.35 = (bf16[768,384]{1,0:T(8,128)(2,1)S(1)}, bf16[768,384]{1,0:T(8,128)(2,1)S(1)}, u32[]{:S(2)}, u32[]{:S(2)}) collective-permute-start(bf16[768,384]{1,0:T(8,128)(2,1)S(1)} %get-tuple-element.815), channel_id=1, source_target_pairs={{0,4},{4,8},{8,12},{12,14},{14,10},{10,6},{6,2},{2,0},{1,5},{5,9},... | collective-permute-start | bytes 1769480 | tf_op jit(solution)/shard_map/ppermute | solution.py:603
  125.7 19.2 %collective-permute-start.37 = (bf16[400,384]{1,0:T(8,128)(2,1)S(1)}, bf16[400,384]{1,0:T(8,128)(2,1)S(1)}, u32[]{:S(2)}, u32[]{:S(2)}) collective-permute-start(bf16[400,384]{1,0:T(8,128)(2,1)S(1)} %get-tuple-element.817), channel_id=1, source_target_pairs={{0,4},{4,8},{8,12},{12,14},{14,10},{10,6},{6,2},{2,0},{1,5},{5,9},... | collective-permute-start | bytes 921608 | tf_op jit(solution)/shard_map/ppermute | solution.py:603
  128.0 18.6 %collective-permute-start.38 = (bf16[400,384]{1,0:T(8,128)(2,1)S(1)}, bf16[400,384]{1,0:T(8,128)(2,1)S(1)}, u32[]{:S(2)}, u32[]{:S(2)}) collective-permute-start(bf16[400,384]{1,0:T(8,128)(2,1)S(1)} %get-tuple-element.816), channel_id=1, source_target_pairs={{4,0},{8,4},{12,8},{14,12},{10,14},{6,10},{2,6},{0,2},{5,1},{9,5},... | collective-permute-start | bytes 921608 | tf_op jit(solution)/shard_map/ppermute | solution.py:603
  141.9 17.3 %collective-permute-start.44 = (bf16[768,384]{1,0:T(8,128)(2,1)S(1)}, bf16[768,384]{1,0:T(8,128)(2,1)S(1)}, u32[]{:S(2)}, u32[]{:S(2)}) collective-permute-start(bf16[768,384]{1,0:T(8,128)(2,1)S(1)} %get-tuple-element.616), channel_id=1, source_target_pairs={{4,0},{8,4},{12,8},{14,12},{10,14},{6,10},{2,6},{0,2},{5,1},{9,5},... | collective-permute-start | bytes 1769480 | tf_op jit(solution)/shard_map/ppermute | solution.py:603
  148.4 17.4 %collective-permute-start.42 = (bf16[400,384]{1,0:T(8,128)(2,1)S(1)}, bf16[400,384]{1,0:T(8,128)(2,1)S(1)}, u32[]{:S(2)}, u32[]{:S(2)}) collective-permute-start(bf16[400,384]{1,0:T(8,128)(2,1)S(1)} %get-tuple-element.614), channel_id=1, source_target_pairs={{4,0},{8,4},{12,8},{14,12},{10,14},{6,10},{2,6},{0,2},{5,1},{9,5},... | collective-permute-start | bytes 921608 | tf_op jit(solution)/shard_map/ppermute | solution.py:603
  167.6 17.4 %collective-permute-start.46 = (bf16[400,384]{1,0:T(8,128)(2,1)S(1)}, bf16[400,384]{1,0:T(8,128)(2,1)S(1)}, u32[]{:S(2)}, u32[]{:S(2)}) collective-permute-start(bf16[400,384]{1,0:T(8,128)(2,1)S(1)} %get-tuple-element.630), channel_id=1, source_target_pairs={{4,0},{8,4},{12,8},{14,12},{10,14},{6,10},{2,6},{0,2},{5,1},{9,5},... | collective-permute-start | bytes 921608 | tf_op jit(solution)/shard_map/ppermute | solution.py:603
  180.4 17.3 %collective-permute-start.52 = (bf16[768,384]{1,0:T(8,128)(2,1)S(1)}, bf16[768,384]{1,0:T(8,128)(2,1)S(1)}, u32[]{:S(2)}, u32[]{:S(2)}) collective-permute-start(bf16[768,384]{1,0:T(8,128)(2,1)S(1)} %get-tuple-element.648), channel_id=1, source_target_pairs={{4,0},{8,4},{12,8},{14,12},{10,14},{6,10},{2,6},{0,2},{5,1},{9,5},... | collective-permute-start | bytes 1769480 | tf_op jit(solution)/shard_map/ppermute | solution.py:603
  185.2 17.6 %collective-permute-start.49 = (bf16[400,384]{1,0:T(8,128)(2,1)S(1)}, bf16[400,384]{1,0:T(8,128)(2,1)S(1)}, u32[]{:S(2)}, u32[]{:S(2)}) collective-permute-start(bf16[400,384]{1,0:T(8,128)(2,1)S(1)} %get-tuple-element.645), channel_id=1, source_target_pairs={{0,4},{4,8},{8,12},{12,14},{14,10},{10,6},{6,2},{2,0},{1,5},{5,9},... | collective-permute-start | bytes 921608 | tf_op jit(solution)/shard_map/ppermute | solution.py:603
  186.8 17.4 %collective-permute-start.50 = (bf16[400,384]{1,0:T(8,128)(2,1)S(1)}, bf16[400,384]{1,0:T(8,128)(2,1)S(1)}, u32[]{:S(2)}, u32[]{:S(2)}) collective-permute-start(bf16[400,384]{1,0:T(8,128)(2,1)S(1)} %get-tuple-element.646), channel_id=1, source_target_pairs={{4,0},{8,4},{12,8},{14,12},{10,14},{6,10},{2,6},{0,2},{5,1},{9,5},... | collective-permute-start | bytes 921608 | tf_op jit(solution)/shard_map/ppermute | solution.py:603
  206.0 17.4 %collective-permute-start.54 = (bf16[400,384]{1,0:T(8,128)(2,1)S(1)}, bf16[400,384]{1,0:T(8,128)(2,1)S(1)}, u32[]{:S(2)}, u32[]{:S(2)}) collective-permute-start(bf16[400,384]{1,0:T(8,128)(2,1)S(1)} %get-tuple-element.662), channel_id=1, source_target_pairs={{4,0},{8,4},{12,8},{14,12},{10,14},{6,10},{2,6},{0,2},{5,1},{9,5},... | collective-permute-start | bytes 921608 | tf_op jit(solution)/shard_map/ppermute | solution.py:603
  225.3 17.4 %collective-permute-start.58 = (bf16[400,384]{1,0:T(8,128)(2,1)S(1)}, bf16[400,384]{1,0:T(8,128)(2,1)S(1)}, u32[]{:S(2)}, u32[]{:S(2)}) collective-permute-start(bf16[400,384]{1,0:T(8,128)(2,1)S(1)} %get-tuple-element.678), channel_id=1, source_target_pairs={{4,0},{8,4},{12,8},{14,12},{10,14},{6,10},{2,6},{0,2},{5,1},{9,5},... | collective-permute-start | bytes 921608 | tf_op jit(solution)/shard_map/ppermute | solution.py:603
  244.5 17.4 %collective-permute-start.62 = (bf16[400,384]{1,0:T(8,128)(2,1)S(1)}, bf16[400,384]{1,0:T(8,128)(2,1)S(1)}, u32[]{:S(2)}, u32[]{:S(2)}) collective-permute-start(bf16[400,384]{1,0:T(8,128)(2,1)S(1)} %get-tuple-element.698), channel_id=1, source_target_pairs={{4,0},{8,4},{12,8},{14,12},{10,14},{6,10},{2,6},{0,2},{5,1},{9,5},... | collective-permute-start | bytes 921608 | tf_op jit(solution)/shard_map/ppermute | solution.py:603
  256.9 17.6 %collective-permute-start.68 = (bf16[768,384]{1,0:T(8,128)(2,1)S(1)}, bf16[768,384]{1,0:T(8,128)(2,1)S(1)}, u32[]{:S(2)}, u32[]{:S(2)}) collective-permute-start(bf16[768,384]{1,0:T(8,128)(2,1)S(1)} %collective-permute-done.64.back), channel_id=1, source_target_pairs={{4,0},{8,4},{12,8},{14,12},{10,14},{6,10},{2,6},{0,2},{5,1},{9,5},... | collective-permute-start | bytes 1769480 | tf_op jit(solution)/shard_map/ppermute | solution.py:603
  263.7 17.4 %collective-permute-start.66 = (bf16[400,384]{1,0:T(8,128)(2,1)S(1)}, bf16[400,384]{1,0:T(8,128)(2,1)S(1)}, u32[]{:S(2)}, u32[]{:S(2)}) collective-permute-start(bf16[400,384]{1,0:T(8,128)(2,1)S(1)} %get-tuple-element.712.back), channel_id=1, source_target_pairs={{4,0},{8,4},{12,8},{14,12},{10,14},{6,10},{2,6},{0,2},{5,1},{9,5},... | collective-permute-start | bytes 921608 | tf_op jit(solution)/shard_map/ppermute | solution.py:603
  276.1 17.6 %collective-permute-start.72 = (bf16[768,384]{1,0:T(8,128)(2,1)S(1)}, bf16[768,384]{1,0:T(8,128)(2,1)S(1)}, u32[]{:S(2)}, u32[]{:S(2)}) collective-permute-start(bf16[768,384]{1,0:T(8,128)(2,1)S(1)} %collective-permute-done.68.back), channel_id=1, source_target_pairs={{4,0},{8,4},{12,8},{14,12},{10,14},{6,10},{2,6},{0,2},{5,1},{9,5},... | collective-permute-start | bytes 1769480 | tf_op jit(solution)/shard_map/ppermute | solution.py:603
  282.7 17.6 %collective-permute-start.70 = (bf16[400,384]{1,0:T(8,128)(2,1)S(1)}, bf16[400,384]{1,0:T(8,128)(2,1)S(1)}, u32[]{:S(2)}, u32[]{:S(2)}) collective-permute-start(bf16[400,384]{1,0:T(8,128)(2,1)S(1)} %collective-permute-done.66.back), channel_id=1, source_target_pairs={{4,0},{8,4},{12,8},{14,12},{10,14},{6,10},{2,6},{0,2},{5,1},{9,5},... | collective-permute-start | bytes 921608 | tf_op jit(solution)/shard_map/ppermute | solution.py:603
  295.4 17.6 %collective-permute-start.76 = (bf16[768,384]{1,0:T(8,128)(2,1)S(1)}, bf16[768,384]{1,0:T(8,128)(2,1)S(1)}, u32[]{:S(2)}, u32[]{:S(2)}) collective-permute-start(bf16[768,384]{1,0:T(8,128)(2,1)S(1)} %collective-permute-done.72.back), channel_id=1, source_target_pairs={{4,0},{8,4},{12,8},{14,12},{10,14},{6,10},{2,6},{0,2},{5,1},{9,5},... | collective-permute-start | bytes 1769480 | tf_op jit(solution)/shard_map/ppermute | solution.py:603
  301.9 17.6 %collective-permute-start.74 = (bf16[400,384]{1,0:T(8,128)(2,1)S(1)}, bf16[400,384]{1,0:T(8,128)(2,1)S(1)}, u32[]{:S(2)}, u32[]{:S(2)}) collective-permute-start(bf16[400,384]{1,0:T(8,128)(2,1)S(1)} %collective-permute-done.70.back), channel_id=1, source_target_pairs={{4,0},{8,4},{12,8},{14,12},{10,14},{6,10},{2,6},{0,2},{5,1},{9,5},... | collective-permute-start | bytes 921608 | tf_op jit(solution)/shard_map/ppermute | solution.py:603
  314.6 17.6 %collective-permute-start.80 = (bf16[768,384]{1,0:T(8,128)(2,1)S(1)}, bf16[768,384]{1,0:T(8,128)(2,1)S(1)}, u32[]{:S(2)}, u32[]{:S(2)}) collective-permute-start(bf16[768,384]{1,0:T(8,128)(2,1)S(1)} %collective-permute-done.76.back), channel_id=1, source_target_pairs={{4,0},{8,4},{12,8},{14,12},{10,14},{6,10},{2,6},{0,2},{5,1},{9,5},... | collective-permute-start | bytes 1769480 | tf_op jit(solution)/shard_map/ppermute | solution.py:603
  321.2 17.6 %collective-permute-start.78 = (bf16[400,384]{1,0:T(8,128)(2,1)S(1)}, bf16[400,384]{1,0:T(8,128)(2,1)S(1)}, u32[]{:S(2)}, u32[]{:S(2)}) collective-permute-start(bf16[400,384]{1,0:T(8,128)(2,1)S(1)} %collective-permute-done.74.back), channel_id=1, source_target_pairs={{4,0},{8,4},{12,8},{14,12},{10,14},{6,10},{2,6},{0,2},{5,1},{9,5},... | collective-permute-start | bytes 921608 | tf_op jit(solution)/shard_map/ppermute | solution.py:603
  333.8 17.6 %collective-permute-start.84 = (bf16[768,384]{1,0:T(8,128)(2,1)S(1)}, bf16[768,384]{1,0:T(8,128)(2,1)S(1)}, u32[]{:S(2)}, u32[]{:S(2)}) collective-permute-start(bf16[768,384]{1,0:T(8,128)(2,1)S(1)} %collective-permute-done.80.back), channel_id=1, source_target_pairs={{4,0},{8,4},{12,8},{14,12},{10,14},{6,10},{2,6},{0,2},{5,1},{9,5},... | collective-permute-start | bytes 1769480 | tf_op jit(solution)/shard_map/ppermute | solution.py:603
  340.4 17.6 %collective-permute-start.82 = (bf16[400,384]{1,0:T(8,128)(2,1)S(1)}, bf16[400,384]{1,0:T(8,128)(2,1)S(1)}, u32[]{:S(2)}, u32[]{:S(2)}) collective-permute-start(bf16[400,384]{1,0:T(8,128)(2,1)S(1)} %collective-permute-done.78.back), channel_id=1, source_target_pairs={{4,0},{8,4},{12,8},{14,12},{10,14},{6,10},{2,6},{0,2},{5,1},{9,5},... | collective-permute-start | bytes 921608 | tf_op jit(solution)/shard_map/ppermute | solution.py:603
  353.0 17.6 %collective-permute-start.88 = (bf16[768,384]{1,0:T(8,128)(2,1)S(1)}, bf16[768,384]{1,0:T(8,128)(2,1)S(1)}, u32[]{:S(2)}, u32[]{:S(2)}) collective-permute-start(bf16[768,384]{1,0:T(8,128)(2,1)S(1)} %collective-permute-done.84.back), channel_id=1, source_target_pairs={{4,0},{8,4},{12,8},{14,12},{10,14},{6,10},{2,6},{0,2},{5,1},{9,5},... | collective-permute-start | bytes 1769480 | tf_op jit(solution)/shard_map/ppermute | solution.py:603
  (135 other events, 1042.5 us)
where the time goes:
time: 403 us; the launch traced here: 395 us
  waiting for transfers between devices  161 us (40%)
  Pallas kernels  133 us (33%)
  starting transfers between devices  89 us (22%)
  local copies, waits for them, and re-layouts  7.02 us (2%)
    ppermute x28, waiting for transfers between devices, send(): lax.ppermute(pair[0], 'dp', self.ahead)  90.2 us
    pallas_call x27, Pallas kernels, run_chains(): pl.pallas_call(call, in_specs=[SMEM] + [VMEM] * (len(ins) + len(held)) +...  52.9 us
    ppermute x28, waiting for transfers between devices, send(): lax.ppermute(pair[1], 'dp', self.back)  52.6 us
    ppermute x28, starting transfers between devices, send(): lax.ppermute(pair[0], 'dp', self.ahead)  47.7 us
    pallas_call x16, Pallas kernels, place_step(): pl.pallas_call(call, grid_spec=pltpu.PrefetchScalarGridSpec(num_scalar_pr...  35.5 us
    pallas_call x16, Pallas kernels, run_weights(): pl.pallas_call(behind(functools.partial(kernel, step + 1, len(lists[0])),...  33.8 us
    ppermute x6, starting transfers between devices, across(): return lax.ppermute(value, 'section', [(0, 1), (1, 0)])  22.6 us
    ppermute x28, starting transfers between devices, send(): lax.ppermute(pair[1], 'dp', self.back)  11.6 us
  transfers between devices with their start and end apart: 94, of which 63 were waited for; matrix products, arithmetic and copies ran while one was open for 1% of the time, Pallas kernels for 31%

commit v1 on v0

--- a/solution.py
+++ b/solution.py
@@ -125,7 +125,7 @@
     cdf = 0.5 * (1.0 + lax.erf(pre * root_half))
     hidden = (pre * cdf).astype(BF)
     outs[0][...] = dot(hidden, down[tag]).astype(BF)
-    outs[1][...] = normal
+    outs[1][...] = normal.astype(BF)
     outs[2][...] = inv_root
     outs[3][...] = low
     outs[4][...] = hidden
@@ -133,7 +133,7 @@
 
 
 def second_norm(normal, part, other, gains, shifts):
-    first = normal[...] * gains[0:1] + shifts[0:1]
+    first = normal[...].astype(F32) * gains[0:1] + shifts[0:1]
     return normalise(first + (part[...].astype(F32) + other[...].astype(F32)))
 
 
@@ -158,13 +158,12 @@
     back = norm_back(grads, second, inv_root, gains[1:2])
     low = back.astype(BF)
     d_pre = (dot(low, down[tag]) * slope[...].astype(F32)).astype(BF)
-    outs[0][...] = back
-    outs[1][...] = dot(d_pre, up[tag]).astype(BF)
-    outs[2][...] = low
-    outs[3][...] = d_pre
-    outs[4][...] = own_part(core, (second * gains[1:2] + shifts[1:2]).astype(BF))
-    add_sums(grads, second, outs[5])
-    outs[6][tag] += jnp.sum(d_pre.astype(F32), axis=0, keepdims=True)
+    outs[0][...] = dot(d_pre, up[tag]).astype(BF)
+    outs[1][...] = low
+    outs[2][...] = d_pre
+    outs[3][...] = own_part(core, (second * gains[1:2] + shifts[1:2]).astype(BF))
+    add_sums(grads, second, outs[4])
+    outs[5][tag] += jnp.sum(d_pre.astype(F32), axis=0, keepdims=True)
 
 
 def attn_back_kernel(
@@ -172,8 +171,9 @@
 ):
     tag = marks[3 + start + chain]
     core = marks[1]
-    grads = back[...] + (part[...].astype(F32) + other[...].astype(F32))
-    back_one = norm_back(grads, normal[...], inv_root[...], gains[0:1])
+    grads = back[...].astype(F32) + (part[...].astype(F32) + other[...].astype(F32))
+    normal = normal[...].astype(F32)
+    back_one = norm_back(grads, normal, inv_root[...], gains[0:1])
     low = back_one.astype(BF)
     d_mixed = dot_rows(low, output[tag]).astype(BF)
     width = d_mixed.shape[1]
@@ -197,12 +197,20 @@
     outs[1][...] = own_part(1 - core, d_rows)
     outs[2][...] = low
     outs[3][...] = jnp.concatenate(blocks, axis=1)
-    add_sums(grads, normal[...], outs[4])
+    add_sums(grads, normal, outs[4])
+
+
+class Marks:
+    def __init__(self, ref):
+        self.rows = ref[...]
+
+    def __getitem__(self, at):
+        return self.rows[0, at]
 
 
 def behind(kernel, taken, ignored):
     def call(marks, *refs):
-        kernel(marks, *refs[:taken], *refs[taken + ignored :])
+        kernel(Marks(marks), *refs[:taken], *refs[taken + ignored :])
 
     return call
 
@@ -210,7 +218,6 @@
 ANY = pl.BlockSpec(memory_space=pl.ANY)
 HBM = pl.BlockSpec(memory_space=pltpu.HBM)
 TOKEN = jax.ShapeDtypeStruct((8, 128), F32)
-TOKEN_BLOCK = pl.BlockSpec((8, 128), lambda *_: (0, 0))
 
 
 def sign_off(token):
@@ -252,15 +259,19 @@
     ]
     for copy in copies:
         copy.start()
-    for at in range(3):
-        marks[at] = places[at]
     for copy in copies[:2]:
         copy.wait()
     token = lax.broadcasted_iota(jnp.int32, live.shape, 1)
+    found = [places[at] for at in range(3)]
+    found += [jnp.where(tags[chain] > 0, 1, 0) for chain in range(chains)]
     for chain in range(chains):
-        marks[3 + chain] = jnp.where(tags[chain] > 0, 1, 0)
         inside = (token >= chain * SEQ) & (token < (chain + 1) * SEQ)
-        marks[3 + chains + chain] = jnp.sum(jnp.where(inside, live[...], 0))
+        found.append(jnp.sum(jnp.where(inside, live[...], 0)))
+    lane = lax.broadcasted_iota(jnp.int32, marks.shape, 1)
+    rows = jnp.zeros(marks.shape, jnp.int32)
+    for at, value in enumerate(found):
+        rows = jnp.where(lane == at, value, rows)
+    marks[...] = rows
     for copy in copies[2:]:
         copy.wait()
 
@@ -272,8 +283,8 @@
     return pl.pallas_call(
         functools.partial(prepare_kernel, chains, count),
         in_specs=[SMEM] + [HBM] * count,
-        out_specs=[SMEM] + [VMEM] * len(arrays),
-        out_shape=[jax.ShapeDtypeStruct((3 + 2 * chains,), jnp.int32)]
+        out_specs=[VMEM] * (1 + len(arrays)),
+        out_shape=[jax.ShapeDtypeStruct((8, 128), jnp.int32)]
         + [jax.ShapeDtypeStruct(a.shape, a.dtype) for a in arrays],
         scratch_shapes=[
             pltpu.SMEM(tags.shape, jnp.int32),
@@ -290,6 +301,7 @@
     skipped = count + len(held) + len(after)
 
     def call(marks, *refs):
+        marks = Marks(marks)
         sign_off(refs[-1])
 
         @pl.when(marks[0] == active)
@@ -300,7 +312,7 @@
 
     return pl.pallas_call(
         call,
-        in_specs=[SMEM] + [VMEM] * (count + len(held)) + [ANY] * len(after),
+        in_specs=[VMEM] * (1 + count + len(held)) + [ANY] * len(after),
         out_specs=[VMEM] * (count + 1),
         out_shape=[jax.ShapeDtypeStruct((a.shape[0], a.shape[2], a.shape[1]), BF) for a in arrays]
         + [TOKEN],
@@ -323,6 +335,7 @@
     skipped = len(ins) + len(held) + len(after)
 
     def call(marks, *refs):
+        marks = Marks(marks)
         *refs, token = refs[: len(ins)] + refs[skipped:]
         sign_off(token)
 
@@ -334,7 +347,7 @@
 
     return pl.pallas_call(
         call,
-        in_specs=[SMEM] + [VMEM] * (len(ins) + len(held)) + [ANY] * len(after),
+        in_specs=[VMEM] * (1 + len(ins) + len(held)) + [ANY] * len(after),
         out_specs=[VMEM] * (len(outs) + 1),
         out_shape=shapes + [TOKEN],
         input_output_aliases=aliases,
@@ -452,7 +465,7 @@
     ins = [a for arrays in lists for a in arrays] + list(rest)
     return pl.pallas_call(
         behind(functools.partial(kernel, step + 1, len(lists[0])), len(ins), len(after)),
-        in_specs=[SMEM] + [VMEM] * len(ins) + [ANY] * len(after),
+        in_specs=[VMEM] * (1 + len(ins)) + [ANY] * len(after),
         out_specs=[VMEM, VMEM],
         out_shape=[jax.ShapeDtypeStruct((2, rows_out, BLOCK), BF), TOKEN],
         compiler_params=pltpu.CompilerParams(vmem_limit_bytes=VMEM_LIMIT),
@@ -545,30 +558,22 @@
 
 def place_step(kernel, name, marks, step, pair, held, after):
     shape = pair[0].shape
-    block = pl.BlockSpec(shape, lambda i, *_: (0, 0))
-
     count = len(held)
 
     def call(marks, ahead, back, *refs):
         refs = refs[count + len(after) :]
         sign_off(refs[count])
-        kernel(step, marks, ahead, back, refs[:count], *refs[count + 1 :])
+        kernel(step, Marks(marks), ahead, back, refs[:count], *refs[count + 1 :])
 
     return pl.pallas_call(
         call,
-        grid_spec=pltpu.PrefetchScalarGridSpec(
-            num_scalar_prefetch=1,
-            grid=(1,),
-            in_specs=[block, block] + [HBM] * count + [ANY] * len(after),
-            out_specs=[HBM] * count + [TOKEN_BLOCK],
-            scratch_shapes=[pltpu.VMEM((2,) + shape, F32), pltpu.SemaphoreType.DMA((4,))],
-        ),
+        in_specs=[VMEM] * 3 + [HBM] * count + [ANY] * len(after),
+        out_specs=[HBM] * count + [VMEM],
+        scratch_shapes=[pltpu.VMEM((2,) + shape, F32), pltpu.SemaphoreType.DMA((4,))],
         out_shape=[jax.ShapeDtypeStruct(h.shape, h.dtype) for h in held] + [TOKEN],
         input_output_aliases={3 + i: i for i in range(count)},
         compiler_params=pltpu.CompilerParams(vmem_limit_bytes=VMEM_LIMIT),
-        cost_estimate=pl.CostEstimate(
-            flops=10**10, bytes_accessed=10**6, transcendentals=0
-        ),
+        cost_estimate=pl.CostEstimate(flops=10**10, bytes_accessed=10**6, transcendentals=0),
         name=name,
     )(marks, *pair, *held, *after)
 
@@ -699,7 +704,7 @@
         ins += [(a, "whole", 0) for a in (gains, shifts, up, bias, down)]
         outs = [
             ("down", (width,), BF, "rows"),
-            ("normal", (width,), F32, "rows"),
+            ("normal", (width,), BF, "rows"),
             ("inv_root", (1,), F32, "rows"),
             ("low", (width,), BF, "rows"),
             ("hidden", (units,), BF, "rows"),
@@ -717,7 +722,6 @@
         ins += [(kept[p]["slope"], "rows", 0)]
         ins += [(turned["up"], "whole", 0), (turned["down"], "whole", 0)]
         outs = [
-            ("back", (width,), F32, "rows"),
             ("part", (width,), BF, "rows"),
             ("d_down", (width,), BF, "rows"),
             ("d_pre", (units,), BF, "rows"),
@@ -731,7 +735,7 @@
         feed[p]["part_other"] = swap(feed[p]["part"])
 
     def attn_back(active, p):
-        ins = [(feed[p][n], "rows", 0) for n in ("back", "part", "part_other")]
+        ins = [(feed[p][n], "rows", 0) for n in ("d_down", "part", "part_other")]
         ins += [(kept[p]["normal"], "rows", 0), (kept[p]["inv_root"], "rows", 0)]
         ins += [(gains, "whole", 0), (kept[p]["joined"], "rows", 0), (kept[p]["probs"], "chain", 0)]
         ins += [(joint, "whole", 0), (output, "whole", 0)]
@@ -801,10 +805,10 @@
         (attn_early, 0),
         (attn_early, 1),
         (feed_early, 0),
-        (turn_weights, 1),
         (hand_on, 0),
         (feed_early, 1),
         (attn_early, 2),
+        (turn_weights, 1),
         (receive, 0),
         (attn_late, 0),
         (hand_on, 1),

time: 403 us -> 390 us (0.968)
  Pallas kernels: 133 us -> 108 us
  waiting for transfers between devices: 161 us -> 180 us
    pallas_call x45, Pallas kernels: 92.2 us -> 70.1 us  [the longest x27 39.4 us: run_chains(): pl.pallas_call(call, in_specs=[VMEM] * (1 + len(ins) + len(held)) + [ANY]...]
    ppermute x28, waiting for transfers between devices: 90.2 us -> 110 us  [send(): lax.ppermute(pair[0], 'dp', self.ahead)]
    ppermute x28, waiting for transfers between devices: 52.6 us -> 42.6 us  [send(): lax.ppermute(pair[1], 'dp', self.back)]
    ppermute x6, waiting for transfers between devices: 11.2 us -> 16.3 us  [across(): return lax.ppermute(value, 'section', [(0, 1), (1, 0)])]
    ppermute x32, waiting for transfers between devices: 6.68 us -> 11.4 us  [swap(): return lax.ppermute(value, 'tensor', [(0, 1), (1, 0)])]
  transfers between devices with their start and end apart: 94 -> 94, of which waited for: 63 -> 71; matrix products, arithmetic and copies ran while one was open for 1% -> 1% of each run, Pallas kernels for 31% -> 26%
where the time goes in v1:
time: 390 us; the launch traced here: 383 us
  waiting for transfers between devices  180 us (46%)
  Pallas kernels  108 us (28%)
  starting transfers between devices  85.8 us (22%)
    ppermute x28, waiting for transfers between devices, send(): lax.ppermute(pair[0], 'dp', self.ahead)  110 us
    ppermute x28, starting transfers between devices, send(): lax.ppermute(pair[0], 'dp', self.ahead)  46.7 us
    ppermute x28, waiting for transfers between devices, send(): lax.ppermute(pair[1], 'dp', self.back)  42.6 us
    pallas_call x27, Pallas kernels, run_chains(): pl.pallas_call(call, in_specs=[VMEM] * (1 + len(ins) + len(held)) + [ANY]...  39.4 us
    pallas_call x16, Pallas kernels, run_weights(): pl.pallas_call(behind(functools.partial(kernel, step + 1, len(lists[0])),...  31.3 us
    pallas_call x16, Pallas kernels, place_step(): pl.pallas_call(call, in_specs=[VMEM] * 3 + [HBM] * count + [ANY] * len(af...  27.7 us
    ppermute x6, starting transfers between devices, across(): return lax.ppermute(value, 'section', [(0, 1), (1, 0)])  20.4 us
    ppermute x6, waiting for transfers between devices, across(): return lax.ppermute(value, 'section', [(0, 1), (1, 0)])  16.3 us
  transfers between devices with their start and end apart: 94, of which 71 were waited for; matrix products, arithmetic and copies ran while one was open for 1% of the time, Pallas kernels for 26%

profile of v1, /device:TPU:0, one launch (start us, length us, event | category | flops | bytes accessed | tf_op | source)
XLA Modules:
  0.0 383.0 jit_solution(14881542365323477523)
XLA Ops:
  1.2 3.1 prepare.1
  34.6 3.6 collective-permute-start.15
  44.7 4.0 %collective-permute-start.14 = (bf16[320,384]{1,0:T(8,128)(2,1)S(1)}, bf16[320,384]{1,0:T(8,128)(2,1)S(1)}, u32[]{:S(2)}, u32[]{:S(2)}) collective-permute-start(bf16[320,384]{1,0:T(8,128)(2,1)S(1)} %add_convert_fusion.2), channel_id=1, source_target_pairs={{0,16},{16,0},{1,17},{17,1},{2,18},{18,2},{3,19},{19,3},{4,20},{20... | collective-permute-start | bytes 737288 | tf_op jit(solution)/shard_map/ppermute | solution.py:756
  60.3 10.3 %collective-permute-start.25 = (bf16[320,384]{1,0:T(8,128)(2,1)S(1)}, bf16[320,384]{1,0:T(8,128)(2,1)S(1)}, u32[]{:S(2)}, u32[]{:S(2)}) collective-permute-start(bf16[320,384]{1,0:T(8,128)(2,1)S(1)} %add_convert_fusion.1), channel_id=1, source_target_pairs={{0,16},{16,0},{1,17},{17,1},{2,18},{18,2},{3,19},{19,3},{4,20},{20... | collective-permute-start | bytes 737288 | tf_op jit(solution)/shard_map/ppermute | solution.py:756
  70.8 6.3 %collective-permute-done.25.refs_5_ = bf16[320,384]{1,0:T(8,128)(2,1)S(1)} collective-permute-done((bf16[320,384]{1,0:T(8,128)(2,1)S(1)}, bf16[320,384]{1,0:T(8,128)(2,1)S(1)}, u32[]{:S(2)}, u32[]{:S(2)}) %collective-permute-start.25) | collective-permute-done | bytes 245792 | tf_op jit(solution)/shard_map/ppermute | solution.py:756
  78.9 3.1 feed_back.10
  82.0 3.5 collective-permute-done.30.refs_5_
  97.3 3.8 attn_back.9
  101.2 4.2 %attn_back.10 = (f32[320,384]{1,0:T(8,128)S(1)}, bf16[320,384]{1,0:T(8,128)(2,1)S(1)}, bf16[320,768]{1,0:T(8,128)(2,1)S(1)}, bf16[320,1152]{1,0:T(8,128)(2,1)S(1...) custom-call(s32[8,128]{1,0:T(8,128)S(1)} %get-tuple-element.406.mark, ...), custom_call_target="tpu_custom_call", output_to_operand_aliasing={{0}: (11, {}), {1}: (12, {}), {2}: (13, {}), {3}: (14, {}),... | custom-call | flops 10000000000 | bytes 10000000 | tf_op jit(solution)/shard_map/attn_back/pallas_call | solution.py:348
  105.4 3.8 attn_back.11
  120.8 6.3 %collective-permute-done.39.refs_0_ = bf16[768,384]{1,0:T(8,128)(2,1)S(1)} collective-permute-done((bf16[768,384]{1,0:T(8,128)(2,1)S(1)}, bf16[768,384]{1,0:T(8,128)(2,1)S(1)}, u32[]{:S(2)}, u32[]{:S(2)}) %collective-permute-start.39) | collective-permute-done | bytes 589856 | tf_op jit(solution)/shard_map/ppermute | solution.py:608
  139.3 7.1 %collective-permute-done.43.refs_0_ = bf16[768,384]{1,0:T(8,128)(2,1)S(1)} collective-permute-done((bf16[768,384]{1,0:T(8,128)(2,1)S(1)}, bf16[768,384]{1,0:T(8,128)(2,1)S(1)}, u32[]{:S(2)}, u32[]{:S(2)}) %collective-permute-start.43) | collective-permute-done | bytes 589856 | tf_op jit(solution)/shard_map/ppermute | solution.py:608
  158.5 7.1 %collective-permute-done.47.refs_0_ = bf16[768,384]{1,0:T(8,128)(2,1)S(1)} collective-permute-done((bf16[768,384]{1,0:T(8,128)(2,1)S(1)}, bf16[768,384]{1,0:T(8,128)(2,1)S(1)}, u32[]{:S(2)}, u32[]{:S(2)}) %collective-permute-start.47) | collective-permute-done | bytes 589856 | tf_op jit(solution)/shard_map/ppermute | solution.py:608
  177.7 7.1 %collective-permute-done.51.refs_0_ = bf16[768,384]{1,0:T(8,128)(2,1)S(1)} collective-permute-done((bf16[768,384]{1,0:T(8,128)(2,1)S(1)}, bf16[768,384]{1,0:T(8,128)(2,1)S(1)}, u32[]{:S(2)}, u32[]{:S(2)}) %collective-permute-start.51) | collective-permute-done | bytes 589856 | tf_op jit(solution)/shard_map/ppermute | solution.py:608
  196.9 7.1 %collective-permute-done.55.refs_0_ = bf16[768,384]{1,0:T(8,128)(2,1)S(1)} collective-permute-done((bf16[768,384]{1,0:T(8,128)(2,1)S(1)}, bf16[768,384]{1,0:T(8,128)(2,1)S(1)}, u32[]{:S(2)}, u32[]{:S(2)}) %collective-permute-start.55) | collective-permute-done | bytes 589856 | tf_op jit(solution)/shard_map/ppermute | solution.py:608
  216.4 6.8 %collective-permute-done.59.refs_0_ = bf16[768,384]{1,0:T(8,128)(2,1)S(1)} collective-permute-done((bf16[768,384]{1,0:T(8,128)(2,1)S(1)}, bf16[768,384]{1,0:T(8,128)(2,1)S(1)}, u32[]{:S(2)}, u32[]{:S(2)}) %collective-permute-start.59) | collective-permute-done | bytes 589856 | tf_op jit(solution)/shard_map/ppermute | solution.py:608
  235.6 6.8 %collective-permute-done.63.ahead = bf16[768,384]{1,0:T(8,128)(2,1)S(1)} collective-permute-done((bf16[768,384]{1,0:T(8,128)(2,1)S(1)}, bf16[768,384]{1,0:T(8,128)(2,1)S(1)}, u32[]{:S(2)}, u32[]{:S(2)}) %collective-permute-start.63) | collective-permute-done | bytes 589856 | tf_op jit(solution)/shard_map/ppermute | solution.py:608
  254.7 7.0 %collective-permute-done.67.ahead = bf16[768,384]{1,0:T(8,128)(2,1)S(1)} collective-permute-done((bf16[768,384]{1,0:T(8,128)(2,1)S(1)}, bf16[768,384]{1,0:T(8,128)(2,1)S(1)}, u32[]{:S(2)}, u32[]{:S(2)}) %collective-permute-start.67) | collective-permute-done | bytes 589856 | tf_op jit(solution)/shard_map/ppermute | solution.py:608
  273.7 7.2 %collective-permute-done.71.ahead = bf16[768,384]{1,0:T(8,128)(2,1)S(1)} collective-permute-done((bf16[768,384]{1,0:T(8,128)(2,1)S(1)}, bf16[768,384]{1,0:T(8,128)(2,1)S(1)}, u32[]{:S(2)}, u32[]{:S(2)}) %collective-permute-start.71) | collective-permute-done | bytes 589856 | tf_op jit(solution)/shard_map/ppermute | solution.py:608
  292.9 7.2 %collective-permute-done.75.ahead = bf16[768,384]{1,0:T(8,128)(2,1)S(1)} collective-permute-done((bf16[768,384]{1,0:T(8,128)(2,1)S(1)}, bf16[768,384]{1,0:T(8,128)(2,1)S(1)}, u32[]{:S(2)}, u32[]{:S(2)}) %collective-permute-start.75) | collective-permute-done | bytes 589856 | tf_op jit(solution)/shard_map/ppermute | solution.py:608
  312.2 7.2 %collective-permute-done.79.ahead = bf16[768,384]{1,0:T(8,128)(2,1)S(1)} collective-permute-done((bf16[768,384]{1,0:T(8,128)(2,1)S(1)}, bf16[768,384]{1,0:T(8,128)(2,1)S(1)}, u32[]{:S(2)}, u32[]{:S(2)}) %collective-permute-start.79) | collective-permute-done | bytes 589856 | tf_op jit(solution)/shard_map/ppermute | solution.py:608
  331.4 7.2 %collective-permute-done.83.ahead = bf16[768,384]{1,0:T(8,128)(2,1)S(1)} collective-permute-done((bf16[768,384]{1,0:T(8,128)(2,1)S(1)}, bf16[768,384]{1,0:T(8,128)(2,1)S(1)}, u32[]{:S(2)}, u32[]{:S(2)}) %collective-permute-start.83) | collective-permute-done | bytes 589856 | tf_op jit(solution)/shard_map/ppermute | solution.py:608
  350.6 7.2 %collective-permute-done.87.ahead = bf16[768,384]{1,0:T(8,128)(2,1)S(1)} collective-permute-done((bf16[768,384]{1,0:T(8,128)(2,1)S(1)}, bf16[768,384]{1,0:T(8,128)(2,1)S(1)}, u32[]{:S(2)}, u32[]{:S(2)}) %collective-permute-start.87) | collective-permute-done | bytes 589856 | tf_op jit(solution)/shard_map/ppermute | solution.py:608
  372.4 4.5 %collective-permute-done.92.ahead = bf16[400,384]{1,0:T(8,128)(2,1)S(1)} collective-permute-done((bf16[400,384]{1,0:T(8,128)(2,1)S(1)}, bf16[400,384]{1,0:T(8,128)(2,1)S(1)}, u32[]{:S(2)}, u32[]{:S(2)}) %collective-permute-start.92) | collective-permute-done | bytes 307232 | tf_op jit(solution)/shard_map/ppermute | solution.py:608
  (371 shorter events, 239.2 us)
Async XLA Ops:
  114.7 19.0 %collective-permute-start.37 = (bf16[400,384]{1,0:T(8,128)(2,1)S(1)}, bf16[400,384]{1,0:T(8,128)(2,1)S(1)}, u32[]{:S(2)}, u32[]{:S(2)}) collective-permute-start(bf16[400,384]{1,0:T(8,128)(2,1)S(1)} %get-tuple-element.805), channel_id=1, source_target_pairs={{0,4},{4,8},{8,12},{12,14},{14,10},{10,6},{6,2},{2,0},{1,5},{5,9},... | collective-permute-start | bytes 921608 | tf_op jit(solution)/shard_map/ppermute | solution.py:608
  116.6 18.7 %collective-permute-start.38 = (bf16[400,384]{1,0:T(8,128)(2,1)S(1)}, bf16[400,384]{1,0:T(8,128)(2,1)S(1)}, u32[]{:S(2)}, u32[]{:S(2)}) collective-permute-start(bf16[400,384]{1,0:T(8,128)(2,1)S(1)} %get-tuple-element.804), channel_id=1, source_target_pairs={{4,0},{8,4},{12,8},{14,12},{10,14},{6,10},{2,6},{0,2},{5,1},{9,5},... | collective-permute-start | bytes 921608 | tf_op jit(solution)/shard_map/ppermute | solution.py:608
  135.4 17.5 %collective-permute-start.41 = (bf16[400,384]{1,0:T(8,128)(2,1)S(1)}, bf16[400,384]{1,0:T(8,128)(2,1)S(1)}, u32[]{:S(2)}, u32[]{:S(2)}) collective-permute-start(bf16[400,384]{1,0:T(8,128)(2,1)S(1)} %get-tuple-element.601), channel_id=1, source_target_pairs={{0,4},{4,8},{8,12},{12,14},{14,10},{10,6},{6,2},{2,0},{1,5},{5,9},... | collective-permute-start | bytes 921608 | tf_op jit(solution)/shard_map/ppermute | solution.py:608
  231.5 17.5 %collective-permute-start.61 = (bf16[400,384]{1,0:T(8,128)(2,1)S(1)}, bf16[400,384]{1,0:T(8,128)(2,1)S(1)}, u32[]{:S(2)}, u32[]{:S(2)}) collective-permute-start(bf16[400,384]{1,0:T(8,128)(2,1)S(1)} %get-tuple-element.685), channel_id=1, source_target_pairs={{0,4},{4,8},{8,12},{12,14},{14,10},{10,6},{6,2},{2,0},{1,5},{5,9},... | collective-permute-start | bytes 921608 | tf_op jit(solution)/shard_map/ppermute | solution.py:608
  244.0 17.7 %collective-permute-start.67 = (bf16[768,384]{1,0:T(8,128)(2,1)S(1)}, bf16[768,384]{1,0:T(8,128)(2,1)S(1)}, u32[]{:S(2)}, u32[]{:S(2)}) collective-permute-start(bf16[768,384]{1,0:T(8,128)(2,1)S(1)} %collective-permute-done.63.ahead), channel_id=1, source_target_pairs={{0,4},{4,8},{8,12},{12,14},{14,10},{10,6},{6,2},{2,0},{1,5},{5,9},... | collective-permute-start | bytes 1769480 | tf_op jit(solution)/shard_map/ppermute | solution.py:608
  245.6 17.6 %collective-permute-start.68 = (bf16[768,384]{1,0:T(8,128)(2,1)S(1)}, bf16[768,384]{1,0:T(8,128)(2,1)S(1)}, u32[]{:S(2)}, u32[]{:S(2)}) collective-permute-start(bf16[768,384]{1,0:T(8,128)(2,1)S(1)} %collective-permute-done.64.back), channel_id=1, source_target_pairs={{4,0},{8,4},{12,8},{14,12},{10,14},{6,10},{2,6},{0,2},{5,1},{9,5},... | collective-permute-start | bytes 1769480 | tf_op jit(solution)/shard_map/ppermute | solution.py:608
  263.3 17.7 %collective-permute-start.71 = (bf16[768,384]{1,0:T(8,128)(2,1)S(1)}, bf16[768,384]{1,0:T(8,128)(2,1)S(1)}, u32[]{:S(2)}, u32[]{:S(2)}) collective-permute-start(bf16[768,384]{1,0:T(8,128)(2,1)S(1)} %collective-permute-done.67.ahead), channel_id=1, source_target_pairs={{0,4},{4,8},{8,12},{12,14},{14,10},{10,6},{6,2},{2,0},{1,5},{5,9},... | collective-permute-start | bytes 1769480 | tf_op jit(solution)/shard_map/ppermute | solution.py:608
  264.8 17.6 %collective-permute-start.72 = (bf16[768,384]{1,0:T(8,128)(2,1)S(1)}, bf16[768,384]{1,0:T(8,128)(2,1)S(1)}, u32[]{:S(2)}, u32[]{:S(2)}) collective-permute-start(bf16[768,384]{1,0:T(8,128)(2,1)S(1)} %collective-permute-done.68.back), channel_id=1, source_target_pairs={{4,0},{8,4},{12,8},{14,12},{10,14},{6,10},{2,6},{0,2},{5,1},{9,5},... | collective-permute-start | bytes 1769480 | tf_op jit(solution)/shard_map/ppermute | solution.py:608
  269.8 17.7 %collective-permute-start.69 = (bf16[400,384]{1,0:T(8,128)(2,1)S(1)}, bf16[400,384]{1,0:T(8,128)(2,1)S(1)}, u32[]{:S(2)}, u32[]{:S(2)}) collective-permute-start(bf16[400,384]{1,0:T(8,128)(2,1)S(1)} %collective-permute-done.65.ahead), channel_id=1, source_target_pairs={{0,4},{4,8},{8,12},{12,14},{14,10},{10,6},{6,2},{2,0},{1,5},{5,9},... | collective-permute-start | bytes 921608 | tf_op jit(solution)/shard_map/ppermute | solution.py:608
  271.4 17.6 %collective-permute-start.70 = (bf16[400,384]{1,0:T(8,128)(2,1)S(1)}, bf16[400,384]{1,0:T(8,128)(2,1)S(1)}, u32[]{:S(2)}, u32[]{:S(2)}) collective-permute-start(bf16[400,384]{1,0:T(8,128)(2,1)S(1)} %collective-permute-done.66.back), channel_id=1, source_target_pairs={{4,0},{8,4},{12,8},{14,12},{10,14},{6,10},{2,6},{0,2},{5,1},{9,5},... | collective-permute-start | bytes 921608 | tf_op jit(solution)/shard_map/ppermute | solution.py:608
  282.5 17.7 %collective-permute-start.75 = (bf16[768,384]{1,0:T(8,128)(2,1)S(1)}, bf16[768,384]{1,0:T(8,128)(2,1)S(1)}, u32[]{:S(2)}, u32[]{:S(2)}) collective-permute-start(bf16[768,384]{1,0:T(8,128)(2,1)S(1)} %collective-permute-done.71.ahead), channel_id=1, source_target_pairs={{0,4},{4,8},{8,12},{12,14},{14,10},{10,6},{6,2},{2,0},{1,5},{5,9},... | collective-permute-start | bytes 1769480 | tf_op jit(solution)/shard_map/ppermute | solution.py:608
  284.1 17.6 %collective-permute-start.76 = (bf16[768,384]{1,0:T(8,128)(2,1)S(1)}, bf16[768,384]{1,0:T(8,128)(2,1)S(1)}, u32[]{:S(2)}, u32[]{:S(2)}) collective-permute-start(bf16[768,384]{1,0:T(8,128)(2,1)S(1)} %collective-permute-done.72.back), channel_id=1, source_target_pairs={{4,0},{8,4},{12,8},{14,12},{10,14},{6,10},{2,6},{0,2},{5,1},{9,5},... | collective-permute-start | bytes 1769480 | tf_op jit(solution)/shard_map/ppermute | solution.py:608
  289.1 17.7 %collective-permute-start.73 = (bf16[400,384]{1,0:T(8,128)(2,1)S(1)}, bf16[400,384]{1,0:T(8,128)(2,1)S(1)}, u32[]{:S(2)}, u32[]{:S(2)}) collective-permute-start(bf16[400,384]{1,0:T(8,128)(2,1)S(1)} %collective-permute-done.69.ahead), channel_id=1, source_target_pairs={{0,4},{4,8},{8,12},{12,14},{14,10},{10,6},{6,2},{2,0},{1,5},{5,9},... | collective-permute-start | bytes 921608 | tf_op jit(solution)/shard_map/ppermute | solution.py:608
  290.6 17.6 %collective-permute-start.74 = (bf16[400,384]{1,0:T(8,128)(2,1)S(1)}, bf16[400,384]{1,0:T(8,128)(2,1)S(1)}, u32[]{:S(2)}, u32[]{:S(2)}) collective-permute-start(bf16[400,384]{1,0:T(8,128)(2,1)S(1)} %collective-permute-done.70.back), channel_id=1, source_target_pairs={{4,0},{8,4},{12,8},{14,12},{10,14},{6,10},{2,6},{0,2},{5,1},{9,5},... | collective-permute-start | bytes 921608 | tf_op jit(solution)/shard_map/ppermute | solution.py:608
  301.7 17.7 %collective-permute-start.79 = (bf16[768,384]{1,0:T(8,128)(2,1)S(1)}, bf16[768,384]{1,0:T(8,128)(2,1)S(1)}, u32[]{:S(2)}, u32[]{:S(2)}) collective-permute-start(bf16[768,384]{1,0:T(8,128)(2,1)S(1)} %collective-permute-done.75.ahead), channel_id=1, source_target_pairs={{0,4},{4,8},{8,12},{12,14},{14,10},{10,6},{6,2},{2,0},{1,5},{5,9},... | collective-permute-start | bytes 1769480 | tf_op jit(solution)/shard_map/ppermute | solution.py:608
  303.3 17.6 %collective-permute-start.80 = (bf16[768,384]{1,0:T(8,128)(2,1)S(1)}, bf16[768,384]{1,0:T(8,128)(2,1)S(1)}, u32[]{:S(2)}, u32[]{:S(2)}) collective-permute-start(bf16[768,384]{1,0:T(8,128)(2,1)S(1)} %collective-permute-done.76.back), channel_id=1, source_target_pairs={{4,0},{8,4},{12,8},{14,12},{10,14},{6,10},{2,6},{0,2},{5,1},{9,5},... | collective-permute-start | bytes 1769480 | tf_op jit(solution)/shard_map/ppermute | solution.py:608
  308.3 17.7 %collective-permute-start.77 = (bf16[400,384]{1,0:T(8,128)(2,1)S(1)}, bf16[400,384]{1,0:T(8,128)(2,1)S(1)}, u32[]{:S(2)}, u32[]{:S(2)}) collective-permute-start(bf16[400,384]{1,0:T(8,128)(2,1)S(1)} %collective-permute-done.73.ahead), channel_id=1, source_target_pairs={{0,4},{4,8},{8,12},{12,14},{14,10},{10,6},{6,2},{2,0},{1,5},{5,9},... | collective-permute-start | bytes 921608 | tf_op jit(solution)/shard_map/ppermute | solution.py:608
  309.9 17.6 %collective-permute-start.78 = (bf16[400,384]{1,0:T(8,128)(2,1)S(1)}, bf16[400,384]{1,0:T(8,128)(2,1)S(1)}, u32[]{:S(2)}, u32[]{:S(2)}) collective-permute-start(bf16[400,384]{1,0:T(8,128)(2,1)S(1)} %collective-permute-done.74.back), channel_id=1, source_target_pairs={{4,0},{8,4},{12,8},{14,12},{10,14},{6,10},{2,6},{0,2},{5,1},{9,5},... | collective-permute-start | bytes 921608 | tf_op jit(solution)/shard_map/ppermute | solution.py:608
  320.9 17.7 %collective-permute-start.83 = (bf16[768,384]{1,0:T(8,128)(2,1)S(1)}, bf16[768,384]{1,0:T(8,128)(2,1)S(1)}, u32[]{:S(2)}, u32[]{:S(2)}) collective-permute-start(bf16[768,384]{1,0:T(8,128)(2,1)S(1)} %collective-permute-done.79.ahead), channel_id=1, source_target_pairs={{0,4},{4,8},{8,12},{12,14},{14,10},{10,6},{6,2},{2,0},{1,5},{5,9},... | collective-permute-start | bytes 1769480 | tf_op jit(solution)/shard_map/ppermute | solution.py:608
  322.5 17.6 %collective-permute-start.84 = (bf16[768,384]{1,0:T(8,128)(2,1)S(1)}, bf16[768,384]{1,0:T(8,128)(2,1)S(1)}, u32[]{:S(2)}, u32[]{:S(2)}) collective-permute-start(bf16[768,384]{1,0:T(8,128)(2,1)S(1)} %collective-permute-done.80.back), channel_id=1, source_target_pairs={{4,0},{8,4},{12,8},{14,12},{10,14},{6,10},{2,6},{0,2},{5,1},{9,5},... | collective-permute-start | bytes 1769480 | tf_op jit(solution)/shard_map/ppermute | solution.py:608
  327.5 17.7 %collective-permute-start.81 = (bf16[400,384]{1,0:T(8,128)(2,1)S(1)}, bf16[400,384]{1,0:T(8,128)(2,1)S(1)}, u32[]{:S(2)}, u32[]{:S(2)}) collective-permute-start(bf16[400,384]{1,0:T(8,128)(2,1)S(1)} %collective-permute-done.77.ahead), channel_id=1, source_target_pairs={{0,4},{4,8},{8,12},{12,14},{14,10},{10,6},{6,2},{2,0},{1,5},{5,9},... | collective-permute-start | bytes 921608 | tf_op jit(solution)/shard_map/ppermute | solution.py:608
  329.1 17.6 %collective-permute-start.82 = (bf16[400,384]{1,0:T(8,128)(2,1)S(1)}, bf16[400,384]{1,0:T(8,128)(2,1)S(1)}, u32[]{:S(2)}, u32[]{:S(2)}) collective-permute-start(bf16[400,384]{1,0:T(8,128)(2,1)S(1)} %collective-permute-done.78.back), channel_id=1, source_target_pairs={{4,0},{8,4},{12,8},{14,12},{10,14},{6,10},{2,6},{0,2},{5,1},{9,5},... | collective-permute-start | bytes 921608 | tf_op jit(solution)/shard_map/ppermute | solution.py:608
  340.1 17.7 %collective-permute-start.87 = (bf16[768,384]{1,0:T(8,128)(2,1)S(1)}, bf16[768,384]{1,0:T(8,128)(2,1)S(1)}, u32[]{:S(2)}, u32[]{:S(2)}) collective-permute-start(bf16[768,384]{1,0:T(8,128)(2,1)S(1)} %collective-permute-done.83.ahead), channel_id=1, source_target_pairs={{0,4},{4,8},{8,12},{12,14},{14,10},{10,6},{6,2},{2,0},{1,5},{5,9},... | collective-permute-start | bytes 1769480 | tf_op jit(solution)/shard_map/ppermute | solution.py:608
  341.7 17.6 %collective-permute-start.88 = (bf16[768,384]{1,0:T(8,128)(2,1)S(1)}, bf16[768,384]{1,0:T(8,128)(2,1)S(1)}, u32[]{:S(2)}, u32[]{:S(2)}) collective-permute-start(bf16[768,384]{1,0:T(8,128)(2,1)S(1)} %collective-permute-done.84.back), channel_id=1, source_target_pairs={{4,0},{8,4},{12,8},{14,12},{10,14},{6,10},{2,6},{0,2},{5,1},{9,5},... | collective-permute-start | bytes 1769480 | tf_op jit(solution)/shard_map/ppermute | solution.py:608
  (122 other events, 1005.0 us)

commit v2 on v1

--- a/solution.py
+++ b/solution.py
@@ -17,6 +17,7 @@
 EPS = 1e-05
 SCALE = HEAD_DIM**-0.5
 VMEM_LIMIT = 7 * 1024 * 1024
+CHAIN_LIMIT = 7 * 1024 * 1024
 
 root_half = 0.7071067811865476
 root_two_pi = 0.3989422804014327
@@ -351,7 +352,7 @@
         out_specs=[VMEM] * (len(outs) + 1),
         out_shape=shapes + [TOKEN],
         input_output_aliases=aliases,
-        compiler_params=pltpu.CompilerParams(vmem_limit_bytes=VMEM_LIMIT),
+        compiler_params=pltpu.CompilerParams(vmem_limit_bytes=CHAIN_LIMIT),
         cost_estimate=pl.CostEstimate(flops=10**10, bytes_accessed=10**7, transcendentals=0),
         name=name,
     )(marks, *[a for a, _, _ in ins], *held, *after)
@@ -501,81 +502,116 @@
     )(*pair, local, *after)
 
 
-def feed_place_kernel(step, marks, ahead, back, outs, wide, sems):
+def feed_place_kernel(steps, marks, pairs, outs, wide, sems):
     down, up = outs
     copies = []
-    for which, (ref, way) in enumerate(((ahead, -1), (back, 1))):
-        spot = ring_spot(marks, step, way)
-        far, near = lax.div(spot, 2), lax.rem(spot, 2)
-        wide[which] = ref[...].astype(F32)
-        copies += [
-            pltpu.make_async_copy(
-                wide.at[which, :BLOCK], down.at[which, span(far), span(near)], sems.at[2 * which]
-            ),
-            pltpu.make_async_copy(
-                wide.at[which, BLOCK:], up.at[which, span(near), span(far)], sems.at[2 * which + 1]
-            ),
-        ]
-        for copy in copies[-2:]:
-            copy.start()
+    for at, (step, pair) in enumerate(zip(steps, pairs)):
+        for which, (ref, way) in enumerate(zip(pair, (-1, 1))):
+            spot = ring_spot(marks, step, way)
+            far, near = lax.div(spot, 2), lax.rem(spot, 2)
+            slot = 2 * at + which
+            wide[slot] = ref[...].astype(F32)
+            copies += [
+                pltpu.make_async_copy(
+                    wide.at[slot, :BLOCK], down.at[which, span(far), span(near)], sems.at[2 * slot]
+                ),
+                pltpu.make_async_copy(
+                    wide.at[slot, BLOCK:], up.at[which, span(near), span(far)], sems.at[2 * slot + 1]
+                ),
+            ]
+            for copy in copies[-2:]:
+                copy.start()
     for copy in copies:
         copy.wait()
 
 
-def attn_place_kernel(step, marks, ahead, back, outs, wide, sems):
+def attn_place_kernel(steps, marks, pairs, outs, wide, sems):
     joint, output, small = outs
-    copies = []
-    for which, (ref, way) in enumerate(((ahead, -1), (back, 1))):
-        spot = ring_spot(marks, step, way)
-        far, near = lax.div(spot, 2), lax.rem(spot, 2)
-        wide[which] = ref[...].astype(F32)
-        wide[which, BLOCK : BLOCK + TAIL // 2] = one_whole(ref[BLOCK:])
-        copy = pltpu.make_async_copy(
-            wide.at[which, BLOCK : BLOCK + TAIL // 2], small.at[which, spot], sems.at[2 + which]
-        )
-        copy.start()
-        copies.append(copy)
-
-        @pl.when(far < 3)
-        def _():
-            copy = pltpu.make_async_copy(
-                wide.at[which, :BLOCK], joint.at[which, far, span(near)], sems.at[which]
+    waits = []
+    for at, (step, pair) in enumerate(zip(steps, pairs)):
+        for which, (ref, way) in enumerate(zip(pair, (-1, 1))):
+            spot = ring_spot(marks, step, way)
+            far, near = lax.div(spot, 2), lax.rem(spot, 2)
+            slot = 2 * at + which
+            wide[slot] = ref[...].astype(F32)
+            wide[slot, BLOCK : BLOCK + TAIL // 2] = one_whole(ref[BLOCK:])
+            tail = pltpu.make_async_copy(
+                wide.at[slot, BLOCK : BLOCK + TAIL // 2],
+                small.at[which, spot],
+                sems.at[2 * slot + 1],
             )
-            copy.start()
-            copy.wait()
-
-        @pl.when(far == 3)
-        def _():
-            copy = pltpu.make_async_copy(
-                wide.at[which, :BLOCK], output.at[which, :, span(near)], sems.at[which]
+            to_joint = pltpu.make_async_copy(
+                wide.at[slot, :BLOCK],
+                joint.at[which, jnp.minimum(far, 2), span(near)],
+                sems.at[2 * slot],
             )
-            copy.start()
-            copy.wait()
-
-    for copy in copies:
-        copy.wait()
-
-
-def place_step(kernel, name, marks, step, pair, held, after):
-    shape = pair[0].shape
+            to_output = pltpu.make_async_copy(
+                wide.at[slot, :BLOCK], output.at[which, :, span(near)], sems.at[2 * slot]
+            )
+            tail.start()
+            pl.when(far < 3)(to_joint.start)
+            pl.when(far == 3)(to_output.start)
+            waits.append((far, tail, to_joint, to_output))
+    for far, tail, to_joint, to_output in waits:
+        tail.wait()
+        pl.when(far < 3)(to_joint.wait)
+        pl.when(far == 3)(to_output.wait)
+
+
+def place_step(kernel, name, marks, steps, pairs, held, after):
+    shape = pairs[0][0].shape
     count = len(held)
-
-    def call(marks, ahead, back, *refs):
-        refs = refs[count + len(after) :]
+    given = 2 * len(pairs)
+
+    def call(marks, *refs):
+        taken = [refs[at : at + 2] for at in range(0, given, 2)]
+        refs = refs[given + count + len(after) :]
         sign_off(refs[count])
-        kernel(step, Marks(marks), ahead, back, refs[:count], *refs[count + 1 :])
+        kernel(steps, Marks(marks), taken, refs[:count], *refs[count + 1 :])
 
     return pl.pallas_call(
         call,
-        in_specs=[VMEM] * 3 + [HBM] * count + [ANY] * len(after),
+        in_specs=[VMEM] * (1 + given) + [HBM] * count + [ANY] * len(after),
         out_specs=[HBM] * count + [VMEM],
-        scratch_shapes=[pltpu.VMEM((2,) + shape, F32), pltpu.SemaphoreType.DMA((4,))],
+        scratch_shapes=[
+            pltpu.VMEM((given,) + shape, F32),
+            pltpu.SemaphoreType.DMA((2 * given,)),
+        ],
         out_shape=[jax.ShapeDtypeStruct(h.shape, h.dtype) for h in held] + [TOKEN],
-        input_output_aliases={3 + i: i for i in range(count)},
+        input_output_aliases={1 + given + i: i for i in range(count)},
         compiler_params=pltpu.CompilerParams(vmem_limit_bytes=VMEM_LIMIT),
         cost_estimate=pl.CostEstimate(flops=10**10, bytes_accessed=10**6, transcendentals=0),
         name=name,
-    )(marks, *pair, *held, *after)
+    )(marks, *[value for pair in pairs for value in pair], *held, *after)
+
+
+def finish(mine, theirs, outputs, after):
+    count = len(mine)
+    rows, half = sum(a.shape[0] for a in mine), mine[0].shape[1]
+
+    def call(*refs):
+        grads, whole, token = refs[3 * count + len(after) :]
+        sign_off(token)
+        at = 0
+        for own, other, output in zip(refs, refs[count:], refs[2 * count : 3 * count]):
+            here = slice(at, at + own.shape[0])
+            grads[here] = own[...] + other[...].astype(F32)
+            whole[here] = output[...]
+            at += own.shape[0]
+
+    return pl.pallas_call(
+        call,
+        in_specs=[VMEM] * (3 * count) + [ANY] * len(after),
+        out_specs=[VMEM] * 3,
+        out_shape=[
+            jax.ShapeDtypeStruct((rows, half), F32),
+            jax.ShapeDtypeStruct((rows, half), BF),
+            TOKEN,
+        ],
+        compiler_params=pltpu.CompilerParams(vmem_limit_bytes=VMEM_LIMIT),
+        cost_estimate=pl.CostEstimate(flops=10**10, bytes_accessed=10**6, transcendentals=0),
+        name="finish",
+    )(*mine, *theirs, *outputs, *after)
 
 
 def unwritten(*shapes):
@@ -749,9 +785,6 @@
         *found, sums["attn"] = run(kernel, "attn_back", active, p, ins, outs, attn[p], ["attn"])
         attn[p].update(zip([o[0] for o in outs], found))
 
-    def input_gradient(p, theirs):
-        return attn[p]["mine"] + swap(theirs).astype(F32)
-
     def across(value):
         return lax.ppermute(value, "section", [(0, 1), (1, 0)])
 
@@ -789,7 +822,8 @@
 
     def attn_first(p):
         attn_back(1, p)
-        sent[p]["back"] = across(input_gradient(p, attn[p]["theirs"]).astype(BF))
+        total = attn[p]["mine"] + swap(attn[p]["theirs"]).astype(F32)
+        sent[p]["back"] = across(total.astype(BF))
 
     def receive_back(p):
         moved = order.after(sent[p]["back"])
@@ -896,6 +930,9 @@
             pair=attn_pair,
             local=attn_local,
             weights=attn_weights,
+            steps=[],
+            pairs=[],
+            joins=True,
             sent=1,
             kernel=attn_place_kernel,
             name="attn_place",
@@ -905,6 +942,9 @@
             pair=feed_pair,
             local=feed_local,
             weights=feed_weights,
+            steps=[],
+            pairs=[],
+            joins=False,
             sent=2,
             kernel=feed_place_kernel,
             name="feed_place",
@@ -924,22 +964,30 @@
         if sent < RING - 1:
             stream["local"] = stream["weights"](sent + 1)
         else:
-            stream["held"] = order.run(
-                place_step,
-                stream["kernel"],
-                stream["name"],
-                marks,
-                sent - RING + 1,
-                pair,
-                stream["held"],
-            )
+            stream["steps"].append(sent - RING + 1)
+            stream["pairs"].append(pair)
+            if sent != 2 * RING - 3 or not stream["joins"]:
+                stream["held"] = order.run(
+                    place_step,
+                    stream["kernel"],
+                    stream["name"],
+                    marks,
+                    tuple(stream["steps"]),
+                    stream["pairs"],
+                    stream["held"],
+                )
+                stream["steps"], stream["pairs"] = [], []
         stream["sent"] += 1
 
     attn_stream, feed_stream = streams
-    input_grads = []
     while attn_stream["pair"] is not None or feed_stream["pair"] is not None:
         if attn_stream["sent"] == 2 * RING - 2:
-            input_grads = [input_gradient(p, order.after(attn[p]["theirs"])) for p in parts]
+            input_grads, layer_outputs = order.run(
+                finish,
+                [attn[p]["mine"] for p in parts],
+                [swap(order.after(attn[p]["theirs"])) for p in parts],
+                [feed[p]["outputs"] for p in parts],
+            )
         if feed_stream["pair"] is not None:
             advance(feed_stream)
         if attn_stream["pair"] is not None:
@@ -947,16 +995,12 @@
     joint_out, output_out, small_out = attn_stream["held"]
     down_out, up_out = feed_stream["held"]
 
-    def whole(pieces):
-        return jnp.concatenate(pieces, axis=0)
-
-    input_grads = whole(input_grads)
     rows = small_out[:, :, 0]
     bias_grad = rows[:, :4].reshape(2, units)
     norm_sums = rows[:, 4:].reshape(2, 2, width)
     counts = small_out[0, 0, 1].reshape(3, 128)[:2, :SYMBOLS]
     return (
-        whole([feed[p]["outputs"] for p in parts])[None],
+        layer_outputs[None],
         input_grads[None],
         joint_out.transpose(0, 2, 1, 3)[None],
         output_out[None],

time: 390 us -> 386 us (0.990)
  Pallas kernels: 108 us -> 103 us
  waiting for transfers between devices: 180 us -> 184 us
    ppermute x28, waiting for transfers between devices: 110 us -> 115 us  [send(): lax.ppermute(pair[0], 'dp', self.ahead)]
    pallas_call x16, Pallas kernels: 27.7 us -> 23.1 us  [the longest x15 21.5 us: place_step(): pl.pallas_call(call, in_specs=[VMEM] * (1 + given) + [HBM] * count + [ANY...]
  transfers between devices with their start and end apart: 94 -> 94, of which waited for: 71 -> 69; matrix products, arithmetic and copies ran while one was open for 1% -> 0% of each run, Pallas kernels for 26% -> 25%
where the time goes in v2:
time: 386 us; the launch traced here: 379 us
  waiting for transfers between devices  184 us (48%)
  Pallas kernels  103 us (27%)
  starting transfers between devices  85.1 us (22%)
  local copies, waits for them, and re-layouts  4.1 us (1%)
    ppermute x28, waiting for transfers between devices, send(): lax.ppermute(pair[0], 'dp', self.ahead)  115 us
    ppermute x28, starting transfers between devices, send(): lax.ppermute(pair[0], 'dp', self.ahead)  46.5 us
    ppermute x28, waiting for transfers between devices, send(): lax.ppermute(pair[1], 'dp', self.back)  42.7 us
    pallas_call x27, Pallas kernels, run_chains(): pl.pallas_call(call, in_specs=[VMEM] * (1 + len(ins) + len(held)) + [ANY]...  39.4 us
    pallas_call x16, Pallas kernels, run_weights(): pl.pallas_call(behind(functools.partial(kernel, step + 1, len(lists[0])),...  31.3 us
    pallas_call x15, Pallas kernels, place_step(): pl.pallas_call(call, in_specs=[VMEM] * (1 + given) + [HBM] * count + [ANY...  21.5 us
    ppermute x6, starting transfers between devices, across(): return lax.ppermute(value, 'section', [(0, 1), (1, 0)])  20 us
    ppermute x6, waiting for transfers between devices, across(): return lax.ppermute(value, 'section', [(0, 1), (1, 0)])  17 us
  transfers between devices with their start and end apart: 94, of which 69 were waited for; matrix products, arithmetic and copies ran while one was open for 0% of the time, Pallas kernels for 25%

profile of v2, /device:TPU:0, one launch (start us, length us, event | category | flops | bytes accessed | tf_op | source)
XLA Modules:
  0.0 379.0 jit_solution(10406157616674047928)
XLA Ops:
  1.2 3.1 prepare.1
  34.6 3.4 collective-permute-start.15
  44.6 3.3 collective-permute-start.14
  59.4 10.1 %collective-permute-start.28 = (bf16[320,384]{1,0:T(8,128)(2,1)S(1)}, bf16[320,384]{1,0:T(8,128)(2,1)S(1)}, u32[]{:S(2)}, u32[]{:S(2)}) collective-permute-start(bf16[320,384]{1,0:T(8,128)(2,1)S(1)} %add_convert_fusion.1), channel_id=1, source_target_pairs={{0,16},{16,0},{1,17},{17,1},{2,18},{18,2},{3,19},{19,3},{4,20},{20... | collective-permute-start | bytes 737288 | tf_op jit(solution)/shard_map/ppermute | solution.py:789
  69.6 6.1 %collective-permute-done.28.refs_5_ = bf16[320,384]{1,0:T(8,128)(2,1)S(1)} collective-permute-done((bf16[320,384]{1,0:T(8,128)(2,1)S(1)}, bf16[320,384]{1,0:T(8,128)(2,1)S(1)}, u32[]{:S(2)}, u32[]{:S(2)}) %collective-permute-start.28) | collective-permute-done | bytes 245792 | tf_op jit(solution)/shard_map/ppermute | solution.py:789
  77.6 3.1 feed_back.10
  80.7 3.5 collective-permute-done.31.refs_5_
  96.1 3.8 attn_back.9
  99.9 4.2 %attn_back.10 = (f32[320,384]{1,0:T(8,128)S(1)}, bf16[320,384]{1,0:T(8,128)(2,1)S(1)}, bf16[320,768]{1,0:T(8,128)(2,1)S(1)}, bf16[320,1152]{1,0:T(8,128)(2,1)S(1...) custom-call(s32[8,128]{1,0:T(8,128)S(1)} %get-tuple-element.405.mark, ...), custom_call_target="tpu_custom_call", output_to_operand_aliasing={{0}: (11, {}), {1}: (12, {}), {2}: (13, {}), {3}: (14, {}),... | custom-call | flops 10000000000 | bytes 10000000 | tf_op jit(solution)/shard_map/attn_back/pallas_call | solution.py:349
  104.1 3.7 attn_back.11
  119.5 6.3 %collective-permute-done.39.refs_0_ = bf16[768,384]{1,0:T(8,128)(2,1)S(1)} collective-permute-done((bf16[768,384]{1,0:T(8,128)(2,1)S(1)}, bf16[768,384]{1,0:T(8,128)(2,1)S(1)}, u32[]{:S(2)}, u32[]{:S(2)}) %collective-permute-start.39) | collective-permute-done | bytes 589856 | tf_op jit(solution)/shard_map/ppermute | solution.py:644
  138.0 7.1 %collective-permute-done.43.refs_0_ = bf16[768,384]{1,0:T(8,128)(2,1)S(1)} collective-permute-done((bf16[768,384]{1,0:T(8,128)(2,1)S(1)}, bf16[768,384]{1,0:T(8,128)(2,1)S(1)}, u32[]{:S(2)}, u32[]{:S(2)}) %collective-permute-start.43) | collective-permute-done | bytes 589856 | tf_op jit(solution)/shard_map/ppermute | solution.py:644
  157.2 7.1 %collective-permute-done.47.refs_0_ = bf16[768,384]{1,0:T(8,128)(2,1)S(1)} collective-permute-done((bf16[768,384]{1,0:T(8,128)(2,1)S(1)}, bf16[768,384]{1,0:T(8,128)(2,1)S(1)}, u32[]{:S(2)}, u32[]{:S(2)}) %collective-permute-start.47) | collective-permute-done | bytes 589856 | tf_op jit(solution)/shard_map/ppermute | solution.py:644
  176.4 7.1 %collective-permute-done.51.refs_0_ = bf16[768,384]{1,0:T(8,128)(2,1)S(1)} collective-permute-done((bf16[768,384]{1,0:T(8,128)(2,1)S(1)}, bf16[768,384]{1,0:T(8,128)(2,1)S(1)}, u32[]{:S(2)}, u32[]{:S(2)}) %collective-permute-start.51) | collective-permute-done | bytes 589856 | tf_op jit(solution)/shard_map/ppermute | solution.py:644
  195.6 7.1 %collective-permute-done.55.refs_0_ = bf16[768,384]{1,0:T(8,128)(2,1)S(1)} collective-permute-done((bf16[768,384]{1,0:T(8,128)(2,1)S(1)}, bf16[768,384]{1,0:T(8,128)(2,1)S(1)}, u32[]{:S(2)}, u32[]{:S(2)}) %collective-permute-start.55) | collective-permute-done | bytes 589856 | tf_op jit(solution)/shard_map/ppermute | solution.py:644
  215.1 6.8 %collective-permute-done.59.refs_0_ = bf16[768,384]{1,0:T(8,128)(2,1)S(1)} collective-permute-done((bf16[768,384]{1,0:T(8,128)(2,1)S(1)}, bf16[768,384]{1,0:T(8,128)(2,1)S(1)}, u32[]{:S(2)}, u32[]{:S(2)}) %collective-permute-start.59) | collective-permute-done | bytes 589856 | tf_op jit(solution)/shard_map/ppermute | solution.py:644
  234.3 6.8 %collective-permute-done.63.refs_0_ = bf16[768,384]{1,0:T(8,128)(2,1)S(1)} collective-permute-done((bf16[768,384]{1,0:T(8,128)(2,1)S(1)}, bf16[768,384]{1,0:T(8,128)(2,1)S(1)}, u32[]{:S(2)}, u32[]{:S(2)}) %collective-permute-start.63) | collective-permute-done | bytes 589856 | tf_op jit(solution)/shard_map/ppermute | solution.py:644
  252.7 7.6 %collective-permute-done.67.refs_0_ = bf16[768,384]{1,0:T(8,128)(2,1)S(1)} collective-permute-done((bf16[768,384]{1,0:T(8,128)(2,1)S(1)}, bf16[768,384]{1,0:T(8,128)(2,1)S(1)}, u32[]{:S(2)}, u32[]{:S(2)}) %collective-permute-start.67) | collective-permute-done | bytes 589856 | tf_op jit(solution)/shard_map/ppermute | solution.py:644
  271.8 7.9 %collective-permute-done.71.refs_0_ = bf16[768,384]{1,0:T(8,128)(2,1)S(1)} collective-permute-done((bf16[768,384]{1,0:T(8,128)(2,1)S(1)}, bf16[768,384]{1,0:T(8,128)(2,1)S(1)}, u32[]{:S(2)}, u32[]{:S(2)}) %collective-permute-start.71) | collective-permute-done | bytes 589856 | tf_op jit(solution)/shard_map/ppermute | solution.py:644
  291.0 7.9 %collective-permute-done.75.refs_0_ = bf16[768,384]{1,0:T(8,128)(2,1)S(1)} collective-permute-done((bf16[768,384]{1,0:T(8,128)(2,1)S(1)}, bf16[768,384]{1,0:T(8,128)(2,1)S(1)}, u32[]{:S(2)}, u32[]{:S(2)}) %collective-permute-start.75) | collective-permute-done | bytes 589856 | tf_op jit(solution)/shard_map/ppermute | solution.py:644
  310.2 7.9 %collective-permute-done.79.refs_0_ = bf16[768,384]{1,0:T(8,128)(2,1)S(1)} collective-permute-done((bf16[768,384]{1,0:T(8,128)(2,1)S(1)}, bf16[768,384]{1,0:T(8,128)(2,1)S(1)}, u32[]{:S(2)}, u32[]{:S(2)}) %collective-permute-start.79) | collective-permute-done | bytes 589856 | tf_op jit(solution)/shard_map/ppermute | solution.py:644
  329.4 7.9 %collective-permute-done.83.refs_0_ = bf16[768,384]{1,0:T(8,128)(2,1)S(1)} collective-permute-done((bf16[768,384]{1,0:T(8,128)(2,1)S(1)}, bf16[768,384]{1,0:T(8,128)(2,1)S(1)}, u32[]{:S(2)}, u32[]{:S(2)}) %collective-permute-start.83) | collective-permute-done | bytes 589856 | tf_op jit(solution)/shard_map/ppermute | solution.py:644
  348.6 7.9 %collective-permute-done.87.refs_0_ = bf16[768,384]{1,0:T(8,128)(2,1)S(1)} collective-permute-done((bf16[768,384]{1,0:T(8,128)(2,1)S(1)}, bf16[768,384]{1,0:T(8,128)(2,1)S(1)}, u32[]{:S(2)}, u32[]{:S(2)}) %collective-permute-start.87) | collective-permute-done | bytes 589856 | tf_op jit(solution)/shard_map/ppermute | solution.py:644
  367.1 6.0 %collective-permute-done.92.refs_2_ = bf16[400,384]{1,0:T(8,128)(2,1)S(1)} collective-permute-done((bf16[400,384]{1,0:T(8,128)(2,1)S(1)}, bf16[400,384]{1,0:T(8,128)(2,1)S(1)}, u32[]{:S(2)}, u32[]{:S(2)}) %collective-permute-start.92) | collective-permute-done | bytes 307232 | tf_op jit(solution)/shard_map/ppermute | solution.py:644
  (374 shorter events, 231.0 us)
Async XLA Ops:
  113.4 19.0 %collective-permute-start.37 = (bf16[400,384]{1,0:T(8,128)(2,1)S(1)}, bf16[400,384]{1,0:T(8,128)(2,1)S(1)}, u32[]{:S(2)}, u32[]{:S(2)}) collective-permute-start(bf16[400,384]{1,0:T(8,128)(2,1)S(1)} %get-tuple-element.803), channel_id=1, source_target_pairs={{0,4},{4,8},{8,12},{12,14},{14,10},{10,6},{6,2},{2,0},{1,5},{5,9},... | collective-permute-start | bytes 921608 | tf_op jit(solution)/shard_map/ppermute | solution.py:644
  115.3 18.7 %collective-permute-start.38 = (bf16[400,384]{1,0:T(8,128)(2,1)S(1)}, bf16[400,384]{1,0:T(8,128)(2,1)S(1)}, u32[]{:S(2)}, u32[]{:S(2)}) collective-permute-start(bf16[400,384]{1,0:T(8,128)(2,1)S(1)} %get-tuple-element.802), channel_id=1, source_target_pairs={{4,0},{8,4},{12,8},{14,12},{10,14},{6,10},{2,6},{0,2},{5,1},{9,5},... | collective-permute-start | bytes 921608 | tf_op jit(solution)/shard_map/ppermute | solution.py:644
  134.1 17.5 %collective-permute-start.41 = (bf16[400,384]{1,0:T(8,128)(2,1)S(1)}, bf16[400,384]{1,0:T(8,128)(2,1)S(1)}, u32[]{:S(2)}, u32[]{:S(2)}) collective-permute-start(bf16[400,384]{1,0:T(8,128)(2,1)S(1)} %get-tuple-element.599), channel_id=1, source_target_pairs={{0,4},{4,8},{8,12},{12,14},{14,10},{10,6},{6,2},{2,0},{1,5},{5,9},... | collective-permute-start | bytes 921608 | tf_op jit(solution)/shard_map/ppermute | solution.py:644
  230.3 17.5 %collective-permute-start.61 = (bf16[400,384]{1,0:T(8,128)(2,1)S(1)}, bf16[400,384]{1,0:T(8,128)(2,1)S(1)}, u32[]{:S(2)}, u32[]{:S(2)}) collective-permute-start(bf16[400,384]{1,0:T(8,128)(2,1)S(1)} %get-tuple-element.683), channel_id=1, source_target_pairs={{0,4},{4,8},{8,12},{12,14},{14,10},{10,6},{6,2},{2,0},{1,5},{5,9},... | collective-permute-start | bytes 921608 | tf_op jit(solution)/shard_map/ppermute | solution.py:644
  242.7 17.6 %collective-permute-start.67 = (bf16[768,384]{1,0:T(8,128)(2,1)S(1)}, bf16[768,384]{1,0:T(8,128)(2,1)S(1)}, u32[]{:S(2)}, u32[]{:S(2)}) collective-permute-start(bf16[768,384]{1,0:T(8,128)(2,1)S(1)} %collective-permute-done.63.refs_0_), channel_id=1, source_target_pairs={{0,4},{4,8},{8,12},{12,14},{14,10},{10,6},{6,2},{2,0},{1,5},{5,9},... | collective-permute-start | bytes 1769480 | tf_op jit(solution)/shard_map/ppermute | solution.py:644
  244.3 17.6 %collective-permute-start.68 = (bf16[768,384]{1,0:T(8,128)(2,1)S(1)}, bf16[768,384]{1,0:T(8,128)(2,1)S(1)}, u32[]{:S(2)}, u32[]{:S(2)}) collective-permute-start(bf16[768,384]{1,0:T(8,128)(2,1)S(1)} %collective-permute-done.64.refs_1_), channel_id=1, source_target_pairs={{4,0},{8,4},{12,8},{14,12},{10,14},{6,10},{2,6},{0,2},{5,1},{9,5},... | collective-permute-start | bytes 1769480 | tf_op jit(solution)/shard_map/ppermute | solution.py:644
  262.0 17.6 %collective-permute-start.71 = (bf16[768,384]{1,0:T(8,128)(2,1)S(1)}, bf16[768,384]{1,0:T(8,128)(2,1)S(1)}, u32[]{:S(2)}, u32[]{:S(2)}) collective-permute-start(bf16[768,384]{1,0:T(8,128)(2,1)S(1)} %collective-permute-done.67.refs_0_), channel_id=1, source_target_pairs={{0,4},{4,8},{8,12},{12,14},{14,10},{10,6},{6,2},{2,0},{1,5},{5,9},... | collective-permute-start | bytes 1769480 | tf_op jit(solution)/shard_map/ppermute | solution.py:644
  263.5 17.6 %collective-permute-start.72 = (bf16[768,384]{1,0:T(8,128)(2,1)S(1)}, bf16[768,384]{1,0:T(8,128)(2,1)S(1)}, u32[]{:S(2)}, u32[]{:S(2)}) collective-permute-start(bf16[768,384]{1,0:T(8,128)(2,1)S(1)} %collective-permute-done.68.refs_1_), channel_id=1, source_target_pairs={{4,0},{8,4},{12,8},{14,12},{10,14},{6,10},{2,6},{0,2},{5,1},{9,5},... | collective-permute-start | bytes 1769480 | tf_op jit(solution)/shard_map/ppermute | solution.py:644
  268.5 17.6 %collective-permute-start.69 = (bf16[400,384]{1,0:T(8,128)(2,1)S(1)}, bf16[400,384]{1,0:T(8,128)(2,1)S(1)}, u32[]{:S(2)}, u32[]{:S(2)}) collective-permute-start(bf16[400,384]{1,0:T(8,128)(2,1)S(1)} %collective-permute-done.65.refs_0_), channel_id=1, source_target_pairs={{0,4},{4,8},{8,12},{12,14},{14,10},{10,6},{6,2},{2,0},{1,5},{5,9},... | collective-permute-start | bytes 921608 | tf_op jit(solution)/shard_map/ppermute | solution.py:644
  270.1 17.6 %collective-permute-start.70 = (bf16[400,384]{1,0:T(8,128)(2,1)S(1)}, bf16[400,384]{1,0:T(8,128)(2,1)S(1)}, u32[]{:S(2)}, u32[]{:S(2)}) collective-permute-start(bf16[400,384]{1,0:T(8,128)(2,1)S(1)} %collective-permute-done.66.refs_1_), channel_id=1, source_target_pairs={{4,0},{8,4},{12,8},{14,12},{10,14},{6,10},{2,6},{0,2},{5,1},{9,5},... | collective-permute-start | bytes 921608 | tf_op jit(solution)/shard_map/ppermute | solution.py:644
  281.2 17.6 %collective-permute-start.75 = (bf16[768,384]{1,0:T(8,128)(2,1)S(1)}, bf16[768,384]{1,0:T(8,128)(2,1)S(1)}, u32[]{:S(2)}, u32[]{:S(2)}) collective-permute-start(bf16[768,384]{1,0:T(8,128)(2,1)S(1)} %collective-permute-done.71.refs_0_), channel_id=1, source_target_pairs={{0,4},{4,8},{8,12},{12,14},{14,10},{10,6},{6,2},{2,0},{1,5},{5,9},... | collective-permute-start | bytes 1769480 | tf_op jit(solution)/shard_map/ppermute | solution.py:644
  282.8 17.6 %collective-permute-start.76 = (bf16[768,384]{1,0:T(8,128)(2,1)S(1)}, bf16[768,384]{1,0:T(8,128)(2,1)S(1)}, u32[]{:S(2)}, u32[]{:S(2)}) collective-permute-start(bf16[768,384]{1,0:T(8,128)(2,1)S(1)} %collective-permute-done.72.refs_1_), channel_id=1, source_target_pairs={{4,0},{8,4},{12,8},{14,12},{10,14},{6,10},{2,6},{0,2},{5,1},{9,5},... | collective-permute-start | bytes 1769480 | tf_op jit(solution)/shard_map/ppermute | solution.py:644
  287.8 17.6 %collective-permute-start.73 = (bf16[400,384]{1,0:T(8,128)(2,1)S(1)}, bf16[400,384]{1,0:T(8,128)(2,1)S(1)}, u32[]{:S(2)}, u32[]{:S(2)}) collective-permute-start(bf16[400,384]{1,0:T(8,128)(2,1)S(1)} %collective-permute-done.69.refs_0_), channel_id=1, source_target_pairs={{0,4},{4,8},{8,12},{12,14},{14,10},{10,6},{6,2},{2,0},{1,5},{5,9},... | collective-permute-start | bytes 921608 | tf_op jit(solution)/shard_map/ppermute | solution.py:644
  289.3 17.6 %collective-permute-start.74 = (bf16[400,384]{1,0:T(8,128)(2,1)S(1)}, bf16[400,384]{1,0:T(8,128)(2,1)S(1)}, u32[]{:S(2)}, u32[]{:S(2)}) collective-permute-start(bf16[400,384]{1,0:T(8,128)(2,1)S(1)} %collective-permute-done.70.refs_1_), channel_id=1, source_target_pairs={{4,0},{8,4},{12,8},{14,12},{10,14},{6,10},{2,6},{0,2},{5,1},{9,5},... | collective-permute-start | bytes 921608 | tf_op jit(solution)/shard_map/ppermute | solution.py:644
  300.4 17.6 %collective-permute-start.79 = (bf16[768,384]{1,0:T(8,128)(2,1)S(1)}, bf16[768,384]{1,0:T(8,128)(2,1)S(1)}, u32[]{:S(2)}, u32[]{:S(2)}) collective-permute-start(bf16[768,384]{1,0:T(8,128)(2,1)S(1)} %collective-permute-done.75.refs_0_), channel_id=1, source_target_pairs={{0,4},{4,8},{8,12},{12,14},{14,10},{10,6},{6,2},{2,0},{1,5},{5,9},... | collective-permute-start | bytes 1769480 | tf_op jit(solution)/shard_map/ppermute | solution.py:644
  302.0 17.6 %collective-permute-start.80 = (bf16[768,384]{1,0:T(8,128)(2,1)S(1)}, bf16[768,384]{1,0:T(8,128)(2,1)S(1)}, u32[]{:S(2)}, u32[]{:S(2)}) collective-permute-start(bf16[768,384]{1,0:T(8,128)(2,1)S(1)} %collective-permute-done.76.refs_1_), channel_id=1, source_target_pairs={{4,0},{8,4},{12,8},{14,12},{10,14},{6,10},{2,6},{0,2},{5,1},{9,5},... | collective-permute-start | bytes 1769480 | tf_op jit(solution)/shard_map/ppermute | solution.py:644
  307.0 17.6 %collective-permute-start.77 = (bf16[400,384]{1,0:T(8,128)(2,1)S(1)}, bf16[400,384]{1,0:T(8,128)(2,1)S(1)}, u32[]{:S(2)}, u32[]{:S(2)}) collective-permute-start(bf16[400,384]{1,0:T(8,128)(2,1)S(1)} %collective-permute-done.73.refs_0_), channel_id=1, source_target_pairs={{0,4},{4,8},{8,12},{12,14},{14,10},{10,6},{6,2},{2,0},{1,5},{5,9},... | collective-permute-start | bytes 921608 | tf_op jit(solution)/shard_map/ppermute | solution.py:644
  308.6 17.6 %collective-permute-start.78 = (bf16[400,384]{1,0:T(8,128)(2,1)S(1)}, bf16[400,384]{1,0:T(8,128)(2,1)S(1)}, u32[]{:S(2)}, u32[]{:S(2)}) collective-permute-start(bf16[400,384]{1,0:T(8,128)(2,1)S(1)} %collective-permute-done.74.refs_1_), channel_id=1, source_target_pairs={{4,0},{8,4},{12,8},{14,12},{10,14},{6,10},{2,6},{0,2},{5,1},{9,5},... | collective-permute-start | bytes 921608 | tf_op jit(solution)/shard_map/ppermute | solution.py:644
  319.6 17.6 %collective-permute-start.83 = (bf16[768,384]{1,0:T(8,128)(2,1)S(1)}, bf16[768,384]{1,0:T(8,128)(2,1)S(1)}, u32[]{:S(2)}, u32[]{:S(2)}) collective-permute-start(bf16[768,384]{1,0:T(8,128)(2,1)S(1)} %collective-permute-done.79.refs_0_), channel_id=1, source_target_pairs={{0,4},{4,8},{8,12},{12,14},{14,10},{10,6},{6,2},{2,0},{1,5},{5,9},... | collective-permute-start | bytes 1769480 | tf_op jit(solution)/shard_map/ppermute | solution.py:644
  321.2 17.6 %collective-permute-start.84 = (bf16[768,384]{1,0:T(8,128)(2,1)S(1)}, bf16[768,384]{1,0:T(8,128)(2,1)S(1)}, u32[]{:S(2)}, u32[]{:S(2)}) collective-permute-start(bf16[768,384]{1,0:T(8,128)(2,1)S(1)} %collective-permute-done.80.refs_1_), channel_id=1, source_target_pairs={{4,0},{8,4},{12,8},{14,12},{10,14},{6,10},{2,6},{0,2},{5,1},{9,5},... | collective-permute-start | bytes 1769480 | tf_op jit(solution)/shard_map/ppermute | solution.py:644
  326.2 17.6 %collective-permute-start.81 = (bf16[400,384]{1,0:T(8,128)(2,1)S(1)}, bf16[400,384]{1,0:T(8,128)(2,1)S(1)}, u32[]{:S(2)}, u32[]{:S(2)}) collective-permute-start(bf16[400,384]{1,0:T(8,128)(2,1)S(1)} %collective-permute-done.77.refs_0_), channel_id=1, source_target_pairs={{0,4},{4,8},{8,12},{12,14},{14,10},{10,6},{6,2},{2,0},{1,5},{5,9},... | collective-permute-start | bytes 921608 | tf_op jit(solution)/shard_map/ppermute | solution.py:644
  327.8 17.6 %collective-permute-start.82 = (bf16[400,384]{1,0:T(8,128)(2,1)S(1)}, bf16[400,384]{1,0:T(8,128)(2,1)S(1)}, u32[]{:S(2)}, u32[]{:S(2)}) collective-permute-start(bf16[400,384]{1,0:T(8,128)(2,1)S(1)} %collective-permute-done.78.refs_1_), channel_id=1, source_target_pairs={{4,0},{8,4},{12,8},{14,12},{10,14},{6,10},{2,6},{0,2},{5,1},{9,5},... | collective-permute-start | bytes 921608 | tf_op jit(solution)/shard_map/ppermute | solution.py:644
  338.9 17.6 %collective-permute-start.87 = (bf16[768,384]{1,0:T(8,128)(2,1)S(1)}, bf16[768,384]{1,0:T(8,128)(2,1)S(1)}, u32[]{:S(2)}, u32[]{:S(2)}) collective-permute-start(bf16[768,384]{1,0:T(8,128)(2,1)S(1)} %collective-permute-done.83.refs_0_), channel_id=1, source_target_pairs={{0,4},{4,8},{8,12},{12,14},{14,10},{10,6},{6,2},{2,0},{1,5},{5,9},... | collective-permute-start | bytes 1769480 | tf_op jit(solution)/shard_map/ppermute | solution.py:644
  340.4 17.6 %collective-permute-start.88 = (bf16[768,384]{1,0:T(8,128)(2,1)S(1)}, bf16[768,384]{1,0:T(8,128)(2,1)S(1)}, u32[]{:S(2)}, u32[]{:S(2)}) collective-permute-start(bf16[768,384]{1,0:T(8,128)(2,1)S(1)} %collective-permute-done.84.refs_1_), channel_id=1, source_target_pairs={{4,0},{8,4},{12,8},{14,12},{10,14},{6,10},{2,6},{0,2},{5,1},{9,5},... | collective-permute-start | bytes 1769480 | tf_op jit(solution)/shard_map/ppermute | solution.py:644
  (126 other events, 1036.3 us)

commit v3 on v2

--- a/solution.py
+++ b/solution.py
@@ -851,8 +851,8 @@
         (feed_first, 0),
         (hand_on, 2),
         (receive, 1),
+        (attn_late, 1),
         (attn_first, 0),
-        (attn_late, 1),
         (receive, 2),
         (turn_weights, 0),
         (feed_late, 1),

time: 386 us -> 387 us (level)
  no operation moved by 1% of the time
where the time goes in v3:
time: 387 us; the launch traced here: 379 us
  waiting for transfers between devices  183 us (47%)
  Pallas kernels  103 us (27%)
  starting transfers between devices  84 us (22%)
  local copies, waits for them, and re-layouts  5.67 us (1%)
    ppermute x28, waiting for transfers between devices, send(): lax.ppermute(pair[0], 'dp', self.ahead)  115 us
    ppermute x28, starting transfers between devices, send(): lax.ppermute(pair[0], 'dp', self.ahead)  46.5 us
    ppermute x28, waiting for transfers between devices, send(): lax.ppermute(pair[1], 'dp', self.back)  42.6 us
    pallas_call x27, Pallas kernels, run_chains(): pl.pallas_call(call, in_specs=[VMEM] * (1 + len(ins) + len(held)) + [ANY]...  39.3 us
    pallas_call x16, Pallas kernels, run_weights(): pl.pallas_call(behind(functools.partial(kernel, step + 1, len(lists[0])),...  31.3 us
    pallas_call x15, Pallas kernels, place_step(): pl.pallas_call(call, in_specs=[VMEM] * (1 + given) + [HBM] * count + [ANY...  21.5 us
    ppermute x6, starting transfers between devices, across(): return lax.ppermute(value, 'section', [(0, 1), (1, 0)])  18.6 us
    ppermute x6, waiting for transfers between devices, across(): return lax.ppermute(value, 'section', [(0, 1), (1, 0)])  16.9 us
  transfers between devices with their start and end apart: 94, of which 69 were waited for; matrix products, arithmetic and copies ran while one was open for 0% of the time, Pallas kernels for 25%

profile of v3, /device:TPU:0, one launch (start us, length us, event | category | flops | bytes accessed | tf_op | source)
XLA Modules:
  0.0 379.1 jit_solution(6452815277654001794)
XLA Ops:
  1.2 3.1 prepare.1
  44.6 4.6 %collective-permute-start.16 = (bf16[320,384]{1,0:T(8,128)(2,1)S(1)}, bf16[320,384]{1,0:T(8,128)(2,1)S(1)}, u32[]{:S(2)}, u32[]{:S(2)}) collective-permute-start(bf16[320,384]{1,0:T(8,128)(2,1)S(1)} %add_convert_fusion.2), channel_id=1, source_target_pairs={{0,16},{16,0},{1,17},{17,1},{2,18},{18,2},{3,19},{19,3},{4,20},{20... | collective-permute-start | bytes 737288 | tf_op jit(solution)/shard_map/ppermute | solution.py:789
  52.0 3.7 collective-permute-done.16.refs_5_
  61.0 8.5 %collective-permute-start.28 = (bf16[320,384]{1,0:T(8,128)(2,1)S(1)}, bf16[320,384]{1,0:T(8,128)(2,1)S(1)}, u32[]{:S(2)}, u32[]{:S(2)}) collective-permute-start(bf16[320,384]{1,0:T(8,128)(2,1)S(1)} %add_convert_fusion.1), channel_id=1, source_target_pairs={{0,16},{16,0},{1,17},{17,1},{2,18},{18,2},{3,19},{19,3},{4,20},{20... | collective-permute-start | bytes 737288 | tf_op jit(solution)/shard_map/ppermute | solution.py:789
  70.7 5.1 %collective-permute-done.28.refs_5_ = bf16[320,384]{1,0:T(8,128)(2,1)S(1)} collective-permute-done((bf16[320,384]{1,0:T(8,128)(2,1)S(1)}, bf16[320,384]{1,0:T(8,128)(2,1)S(1)}, u32[]{:S(2)}, u32[]{:S(2)}) %collective-permute-start.28) | collective-permute-done | bytes 245792 | tf_op jit(solution)/shard_map/ppermute | solution.py:789
  77.7 3.1 feed_back.10
  80.8 3.5 collective-permute-done.31.refs_5_
  96.1 3.8 attn_back.9
  99.9 4.2 %attn_back.10 = (f32[320,384]{1,0:T(8,128)S(1)}, bf16[320,384]{1,0:T(8,128)(2,1)S(1)}, bf16[320,768]{1,0:T(8,128)(2,1)S(1)}, bf16[320,1152]{1,0:T(8,128)(2,1)S(1...) custom-call(s32[8,128]{1,0:T(8,128)S(1)} %get-tuple-element.405.mark, ...), custom_call_target="tpu_custom_call", output_to_operand_aliasing={{0}: (11, {}), {1}: (12, {}), {2}: (13, {}), {3}: (14, {}),... | custom-call | flops 10000000000 | bytes 10000000 | tf_op jit(solution)/shard_map/attn_back/pallas_call | solution.py:349
  104.2 3.7 attn_back.11
  119.6 6.3 %collective-permute-done.39.refs_0_ = bf16[768,384]{1,0:T(8,128)(2,1)S(1)} collective-permute-done((bf16[768,384]{1,0:T(8,128)(2,1)S(1)}, bf16[768,384]{1,0:T(8,128)(2,1)S(1)}, u32[]{:S(2)}, u32[]{:S(2)}) %collective-permute-start.39) | collective-permute-done | bytes 589856 | tf_op jit(solution)/shard_map/ppermute | solution.py:644
  138.0 7.1 %collective-permute-done.43.refs_0_ = bf16[768,384]{1,0:T(8,128)(2,1)S(1)} collective-permute-done((bf16[768,384]{1,0:T(8,128)(2,1)S(1)}, bf16[768,384]{1,0:T(8,128)(2,1)S(1)}, u32[]{:S(2)}, u32[]{:S(2)}) %collective-permute-start.43) | collective-permute-done | bytes 589856 | tf_op jit(solution)/shard_map/ppermute | solution.py:644
  157.3 7.1 %collective-permute-done.47.refs_0_ = bf16[768,384]{1,0:T(8,128)(2,1)S(1)} collective-permute-done((bf16[768,384]{1,0:T(8,128)(2,1)S(1)}, bf16[768,384]{1,0:T(8,128)(2,1)S(1)}, u32[]{:S(2)}, u32[]{:S(2)}) %collective-permute-start.47) | collective-permute-done | bytes 589856 | tf_op jit(solution)/shard_map/ppermute | solution.py:644
  176.5 7.1 %collective-permute-done.51.refs_0_ = bf16[768,384]{1,0:T(8,128)(2,1)S(1)} collective-permute-done((bf16[768,384]{1,0:T(8,128)(2,1)S(1)}, bf16[768,384]{1,0:T(8,128)(2,1)S(1)}, u32[]{:S(2)}, u32[]{:S(2)}) %collective-permute-start.51) | collective-permute-done | bytes 589856 | tf_op jit(solution)/shard_map/ppermute | solution.py:644
  195.7 7.1 %collective-permute-done.55.refs_0_ = bf16[768,384]{1,0:T(8,128)(2,1)S(1)} collective-permute-done((bf16[768,384]{1,0:T(8,128)(2,1)S(1)}, bf16[768,384]{1,0:T(8,128)(2,1)S(1)}, u32[]{:S(2)}, u32[]{:S(2)}) %collective-permute-start.55) | collective-permute-done | bytes 589856 | tf_op jit(solution)/shard_map/ppermute | solution.py:644
  215.2 6.8 %collective-permute-done.59.refs_0_ = bf16[768,384]{1,0:T(8,128)(2,1)S(1)} collective-permute-done((bf16[768,384]{1,0:T(8,128)(2,1)S(1)}, bf16[768,384]{1,0:T(8,128)(2,1)S(1)}, u32[]{:S(2)}, u32[]{:S(2)}) %collective-permute-start.59) | collective-permute-done | bytes 589856 | tf_op jit(solution)/shard_map/ppermute | solution.py:644
  234.4 6.8 %collective-permute-done.63.refs_0_ = bf16[768,384]{1,0:T(8,128)(2,1)S(1)} collective-permute-done((bf16[768,384]{1,0:T(8,128)(2,1)S(1)}, bf16[768,384]{1,0:T(8,128)(2,1)S(1)}, u32[]{:S(2)}, u32[]{:S(2)}) %collective-permute-start.63) | collective-permute-done | bytes 589856 | tf_op jit(solution)/shard_map/ppermute | solution.py:644
  252.8 7.6 %collective-permute-done.67.refs_0_ = bf16[768,384]{1,0:T(8,128)(2,1)S(1)} collective-permute-done((bf16[768,384]{1,0:T(8,128)(2,1)S(1)}, bf16[768,384]{1,0:T(8,128)(2,1)S(1)}, u32[]{:S(2)}, u32[]{:S(2)}) %collective-permute-start.67) | collective-permute-done | bytes 589856 | tf_op jit(solution)/shard_map/ppermute | solution.py:644
  271.8 7.9 %collective-permute-done.71.refs_0_ = bf16[768,384]{1,0:T(8,128)(2,1)S(1)} collective-permute-done((bf16[768,384]{1,0:T(8,128)(2,1)S(1)}, bf16[768,384]{1,0:T(8,128)(2,1)S(1)}, u32[]{:S(2)}, u32[]{:S(2)}) %collective-permute-start.71) | collective-permute-done | bytes 589856 | tf_op jit(solution)/shard_map/ppermute | solution.py:644
  291.0 7.9 %collective-permute-done.75.refs_0_ = bf16[768,384]{1,0:T(8,128)(2,1)S(1)} collective-permute-done((bf16[768,384]{1,0:T(8,128)(2,1)S(1)}, bf16[768,384]{1,0:T(8,128)(2,1)S(1)}, u32[]{:S(2)}, u32[]{:S(2)}) %collective-permute-start.75) | collective-permute-done | bytes 589856 | tf_op jit(solution)/shard_map/ppermute | solution.py:644
  310.3 7.9 %collective-permute-done.79.refs_0_ = bf16[768,384]{1,0:T(8,128)(2,1)S(1)} collective-permute-done((bf16[768,384]{1,0:T(8,128)(2,1)S(1)}, bf16[768,384]{1,0:T(8,128)(2,1)S(1)}, u32[]{:S(2)}, u32[]{:S(2)}) %collective-permute-start.79) | collective-permute-done | bytes 589856 | tf_op jit(solution)/shard_map/ppermute | solution.py:644
  329.5 7.9 %collective-permute-done.83.refs_0_ = bf16[768,384]{1,0:T(8,128)(2,1)S(1)} collective-permute-done((bf16[768,384]{1,0:T(8,128)(2,1)S(1)}, bf16[768,384]{1,0:T(8,128)(2,1)S(1)}, u32[]{:S(2)}, u32[]{:S(2)}) %collective-permute-start.83) | collective-permute-done | bytes 589856 | tf_op jit(solution)/shard_map/ppermute | solution.py:644
  348.7 7.9 %collective-permute-done.87.refs_0_ = bf16[768,384]{1,0:T(8,128)(2,1)S(1)} collective-permute-done((bf16[768,384]{1,0:T(8,128)(2,1)S(1)}, bf16[768,384]{1,0:T(8,128)(2,1)S(1)}, u32[]{:S(2)}, u32[]{:S(2)}) %collective-permute-start.87) | collective-permute-done | bytes 589856 | tf_op jit(solution)/shard_map/ppermute | solution.py:644
  367.2 6.0 %collective-permute-done.92.refs_2_ = bf16[400,384]{1,0:T(8,128)(2,1)S(1)} collective-permute-done((bf16[400,384]{1,0:T(8,128)(2,1)S(1)}, bf16[400,384]{1,0:T(8,128)(2,1)S(1)}, u32[]{:S(2)}, u32[]{:S(2)}) %collective-permute-start.92) | collective-permute-done | bytes 307232 | tf_op jit(solution)/shard_map/ppermute | solution.py:644
  (368 shorter events, 232.0 us)
Async XLA Ops:
  113.5 19.0 %collective-permute-start.37 = (bf16[400,384]{1,0:T(8,128)(2,1)S(1)}, bf16[400,384]{1,0:T(8,128)(2,1)S(1)}, u32[]{:S(2)}, u32[]{:S(2)}) collective-permute-start(bf16[400,384]{1,0:T(8,128)(2,1)S(1)} %get-tuple-element.803), channel_id=1, source_target_pairs={{0,4},{4,8},{8,12},{12,14},{14,10},{10,6},{6,2},{2,0},{1,5},{5,9},... | collective-permute-start | bytes 921608 | tf_op jit(solution)/shard_map/ppermute | solution.py:644
  115.4 18.7 %collective-permute-start.38 = (bf16[400,384]{1,0:T(8,128)(2,1)S(1)}, bf16[400,384]{1,0:T(8,128)(2,1)S(1)}, u32[]{:S(2)}, u32[]{:S(2)}) collective-permute-start(bf16[400,384]{1,0:T(8,128)(2,1)S(1)} %get-tuple-element.802), channel_id=1, source_target_pairs={{4,0},{8,4},{12,8},{14,12},{10,14},{6,10},{2,6},{0,2},{5,1},{9,5},... | collective-permute-start | bytes 921608 | tf_op jit(solution)/shard_map/ppermute | solution.py:644
  134.2 17.5 %collective-permute-start.41 = (bf16[400,384]{1,0:T(8,128)(2,1)S(1)}, bf16[400,384]{1,0:T(8,128)(2,1)S(1)}, u32[]{:S(2)}, u32[]{:S(2)}) collective-permute-start(bf16[400,384]{1,0:T(8,128)(2,1)S(1)} %get-tuple-element.599), channel_id=1, source_target_pairs={{0,4},{4,8},{8,12},{12,14},{14,10},{10,6},{6,2},{2,0},{1,5},{5,9},... | collective-permute-start | bytes 921608 | tf_op jit(solution)/shard_map/ppermute | solution.py:644
  230.3 17.5 %collective-permute-start.61 = (bf16[400,384]{1,0:T(8,128)(2,1)S(1)}, bf16[400,384]{1,0:T(8,128)(2,1)S(1)}, u32[]{:S(2)}, u32[]{:S(2)}) collective-permute-start(bf16[400,384]{1,0:T(8,128)(2,1)S(1)} %get-tuple-element.683), channel_id=1, source_target_pairs={{0,4},{4,8},{8,12},{12,14},{14,10},{10,6},{6,2},{2,0},{1,5},{5,9},... | collective-permute-start | bytes 921608 | tf_op jit(solution)/shard_map/ppermute | solution.py:644
  242.8 17.7 %collective-permute-start.67 = (bf16[768,384]{1,0:T(8,128)(2,1)S(1)}, bf16[768,384]{1,0:T(8,128)(2,1)S(1)}, u32[]{:S(2)}, u32[]{:S(2)}) collective-permute-start(bf16[768,384]{1,0:T(8,128)(2,1)S(1)} %collective-permute-done.63.refs_0_), channel_id=1, source_target_pairs={{0,4},{4,8},{8,12},{12,14},{14,10},{10,6},{6,2},{2,0},{1,5},{5,9},... | collective-permute-start | bytes 1769480 | tf_op jit(solution)/shard_map/ppermute | solution.py:644
  244.4 17.6 %collective-permute-start.68 = (bf16[768,384]{1,0:T(8,128)(2,1)S(1)}, bf16[768,384]{1,0:T(8,128)(2,1)S(1)}, u32[]{:S(2)}, u32[]{:S(2)}) collective-permute-start(bf16[768,384]{1,0:T(8,128)(2,1)S(1)} %collective-permute-done.64.refs_1_), channel_id=1, source_target_pairs={{4,0},{8,4},{12,8},{14,12},{10,14},{6,10},{2,6},{0,2},{5,1},{9,5},... | collective-permute-start | bytes 1769480 | tf_op jit(solution)/shard_map/ppermute | solution.py:644
  262.0 17.7 %collective-permute-start.71 = (bf16[768,384]{1,0:T(8,128)(2,1)S(1)}, bf16[768,384]{1,0:T(8,128)(2,1)S(1)}, u32[]{:S(2)}, u32[]{:S(2)}) collective-permute-start(bf16[768,384]{1,0:T(8,128)(2,1)S(1)} %collective-permute-done.67.refs_0_), channel_id=1, source_target_pairs={{0,4},{4,8},{8,12},{12,14},{14,10},{10,6},{6,2},{2,0},{1,5},{5,9},... | collective-permute-start | bytes 1769480 | tf_op jit(solution)/shard_map/ppermute | solution.py:644
  263.6 17.6 %collective-permute-start.72 = (bf16[768,384]{1,0:T(8,128)(2,1)S(1)}, bf16[768,384]{1,0:T(8,128)(2,1)S(1)}, u32[]{:S(2)}, u32[]{:S(2)}) collective-permute-start(bf16[768,384]{1,0:T(8,128)(2,1)S(1)} %collective-permute-done.68.refs_1_), channel_id=1, source_target_pairs={{4,0},{8,4},{12,8},{14,12},{10,14},{6,10},{2,6},{0,2},{5,1},{9,5},... | collective-permute-start | bytes 1769480 | tf_op jit(solution)/shard_map/ppermute | solution.py:644
  268.6 17.7 %collective-permute-start.69 = (bf16[400,384]{1,0:T(8,128)(2,1)S(1)}, bf16[400,384]{1,0:T(8,128)(2,1)S(1)}, u32[]{:S(2)}, u32[]{:S(2)}) collective-permute-start(bf16[400,384]{1,0:T(8,128)(2,1)S(1)} %collective-permute-done.65.refs_0_), channel_id=1, source_target_pairs={{0,4},{4,8},{8,12},{12,14},{14,10},{10,6},{6,2},{2,0},{1,5},{5,9},... | collective-permute-start | bytes 921608 | tf_op jit(solution)/shard_map/ppermute | solution.py:644
  270.2 17.6 %collective-permute-start.70 = (bf16[400,384]{1,0:T(8,128)(2,1)S(1)}, bf16[400,384]{1,0:T(8,128)(2,1)S(1)}, u32[]{:S(2)}, u32[]{:S(2)}) collective-permute-start(bf16[400,384]{1,0:T(8,128)(2,1)S(1)} %collective-permute-done.66.refs_1_), channel_id=1, source_target_pairs={{4,0},{8,4},{12,8},{14,12},{10,14},{6,10},{2,6},{0,2},{5,1},{9,5},... | collective-permute-start | bytes 921608 | tf_op jit(solution)/shard_map/ppermute | solution.py:644
  281.3 17.7 %collective-permute-start.75 = (bf16[768,384]{1,0:T(8,128)(2,1)S(1)}, bf16[768,384]{1,0:T(8,128)(2,1)S(1)}, u32[]{:S(2)}, u32[]{:S(2)}) collective-permute-start(bf16[768,384]{1,0:T(8,128)(2,1)S(1)} %collective-permute-done.71.refs_0_), channel_id=1, source_target_pairs={{0,4},{4,8},{8,12},{12,14},{14,10},{10,6},{6,2},{2,0},{1,5},{5,9},... | collective-permute-start | bytes 1769480 | tf_op jit(solution)/shard_map/ppermute | solution.py:644
  282.8 17.6 %collective-permute-start.76 = (bf16[768,384]{1,0:T(8,128)(2,1)S(1)}, bf16[768,384]{1,0:T(8,128)(2,1)S(1)}, u32[]{:S(2)}, u32[]{:S(2)}) collective-permute-start(bf16[768,384]{1,0:T(8,128)(2,1)S(1)} %collective-permute-done.72.refs_1_), channel_id=1, source_target_pairs={{4,0},{8,4},{12,8},{14,12},{10,14},{6,10},{2,6},{0,2},{5,1},{9,5},... | collective-permute-start | bytes 1769480 | tf_op jit(solution)/shard_map/ppermute | solution.py:644
  287.8 17.7 %collective-permute-start.73 = (bf16[400,384]{1,0:T(8,128)(2,1)S(1)}, bf16[400,384]{1,0:T(8,128)(2,1)S(1)}, u32[]{:S(2)}, u32[]{:S(2)}) collective-permute-start(bf16[400,384]{1,0:T(8,128)(2,1)S(1)} %collective-permute-done.69.refs_0_), channel_id=1, source_target_pairs={{0,4},{4,8},{8,12},{12,14},{14,10},{10,6},{6,2},{2,0},{1,5},{5,9},... | collective-permute-start | bytes 921608 | tf_op jit(solution)/shard_map/ppermute | solution.py:644
  289.4 17.6 %collective-permute-start.74 = (bf16[400,384]{1,0:T(8,128)(2,1)S(1)}, bf16[400,384]{1,0:T(8,128)(2,1)S(1)}, u32[]{:S(2)}, u32[]{:S(2)}) collective-permute-start(bf16[400,384]{1,0:T(8,128)(2,1)S(1)} %collective-permute-done.70.refs_1_), channel_id=1, source_target_pairs={{4,0},{8,4},{12,8},{14,12},{10,14},{6,10},{2,6},{0,2},{5,1},{9,5},... | collective-permute-start | bytes 921608 | tf_op jit(solution)/shard_map/ppermute | solution.py:644
  300.5 17.7 %collective-permute-start.79 = (bf16[768,384]{1,0:T(8,128)(2,1)S(1)}, bf16[768,384]{1,0:T(8,128)(2,1)S(1)}, u32[]{:S(2)}, u32[]{:S(2)}) collective-permute-start(bf16[768,384]{1,0:T(8,128)(2,1)S(1)} %collective-permute-done.75.refs_0_), channel_id=1, source_target_pairs={{0,4},{4,8},{8,12},{12,14},{14,10},{10,6},{6,2},{2,0},{1,5},{5,9},... | collective-permute-start | bytes 1769480 | tf_op jit(solution)/shard_map/ppermute | solution.py:644
  302.1 17.6 %collective-permute-start.80 = (bf16[768,384]{1,0:T(8,128)(2,1)S(1)}, bf16[768,384]{1,0:T(8,128)(2,1)S(1)}, u32[]{:S(2)}, u32[]{:S(2)}) collective-permute-start(bf16[768,384]{1,0:T(8,128)(2,1)S(1)} %collective-permute-done.76.refs_1_), channel_id=1, source_target_pairs={{4,0},{8,4},{12,8},{14,12},{10,14},{6,10},{2,6},{0,2},{5,1},{9,5},... | collective-permute-start | bytes 1769480 | tf_op jit(solution)/shard_map/ppermute | solution.py:644
  307.1 17.7 %collective-permute-start.77 = (bf16[400,384]{1,0:T(8,128)(2,1)S(1)}, bf16[400,384]{1,0:T(8,128)(2,1)S(1)}, u32[]{:S(2)}, u32[]{:S(2)}) collective-permute-start(bf16[400,384]{1,0:T(8,128)(2,1)S(1)} %collective-permute-done.73.refs_0_), channel_id=1, source_target_pairs={{0,4},{4,8},{8,12},{12,14},{14,10},{10,6},{6,2},{2,0},{1,5},{5,9},... | collective-permute-start | bytes 921608 | tf_op jit(solution)/shard_map/ppermute | solution.py:644
  308.6 17.6 %collective-permute-start.78 = (bf16[400,384]{1,0:T(8,128)(2,1)S(1)}, bf16[400,384]{1,0:T(8,128)(2,1)S(1)}, u32[]{:S(2)}, u32[]{:S(2)}) collective-permute-start(bf16[400,384]{1,0:T(8,128)(2,1)S(1)} %collective-permute-done.74.refs_1_), channel_id=1, source_target_pairs={{4,0},{8,4},{12,8},{14,12},{10,14},{6,10},{2,6},{0,2},{5,1},{9,5},... | collective-permute-start | bytes 921608 | tf_op jit(solution)/shard_map/ppermute | solution.py:644
  319.7 17.7 %collective-permute-start.83 = (bf16[768,384]{1,0:T(8,128)(2,1)S(1)}, bf16[768,384]{1,0:T(8,128)(2,1)S(1)}, u32[]{:S(2)}, u32[]{:S(2)}) collective-permute-start(bf16[768,384]{1,0:T(8,128)(2,1)S(1)} %collective-permute-done.79.refs_0_), channel_id=1, source_target_pairs={{0,4},{4,8},{8,12},{12,14},{14,10},{10,6},{6,2},{2,0},{1,5},{5,9},... | collective-permute-start | bytes 1769480 | tf_op jit(solution)/shard_map/ppermute | solution.py:644
  321.3 17.6 %collective-permute-start.84 = (bf16[768,384]{1,0:T(8,128)(2,1)S(1)}, bf16[768,384]{1,0:T(8,128)(2,1)S(1)}, u32[]{:S(2)}, u32[]{:S(2)}) collective-permute-start(bf16[768,384]{1,0:T(8,128)(2,1)S(1)} %collective-permute-done.80.refs_1_), channel_id=1, source_target_pairs={{4,0},{8,4},{12,8},{14,12},{10,14},{6,10},{2,6},{0,2},{5,1},{9,5},... | collective-permute-start | bytes 1769480 | tf_op jit(solution)/shard_map/ppermute | solution.py:644
  326.3 17.7 %collective-permute-start.81 = (bf16[400,384]{1,0:T(8,128)(2,1)S(1)}, bf16[400,384]{1,0:T(8,128)(2,1)S(1)}, u32[]{:S(2)}, u32[]{:S(2)}) collective-permute-start(bf16[400,384]{1,0:T(8,128)(2,1)S(1)} %collective-permute-done.77.refs_0_), channel_id=1, source_target_pairs={{0,4},{4,8},{8,12},{12,14},{14,10},{10,6},{6,2},{2,0},{1,5},{5,9},... | collective-permute-start | bytes 921608 | tf_op jit(solution)/shard_map/ppermute | solution.py:644
  327.9 17.6 %collective-permute-start.82 = (bf16[400,384]{1,0:T(8,128)(2,1)S(1)}, bf16[400,384]{1,0:T(8,128)(2,1)S(1)}, u32[]{:S(2)}, u32[]{:S(2)}) collective-permute-start(bf16[400,384]{1,0:T(8,128)(2,1)S(1)} %collective-permute-done.78.refs_1_), channel_id=1, source_target_pairs={{4,0},{8,4},{12,8},{14,12},{10,14},{6,10},{2,6},{0,2},{5,1},{9,5},... | collective-permute-start | bytes 921608 | tf_op jit(solution)/shard_map/ppermute | solution.py:644
  338.9 17.7 %collective-permute-start.87 = (bf16[768,384]{1,0:T(8,128)(2,1)S(1)}, bf16[768,384]{1,0:T(8,128)(2,1)S(1)}, u32[]{:S(2)}, u32[]{:S(2)}) collective-permute-start(bf16[768,384]{1,0:T(8,128)(2,1)S(1)} %collective-permute-done.83.refs_0_), channel_id=1, source_target_pairs={{0,4},{4,8},{8,12},{12,14},{14,10},{10,6},{6,2},{2,0},{1,5},{5,9},... | collective-permute-start | bytes 1769480 | tf_op jit(solution)/shard_map/ppermute | solution.py:644
  340.5 17.6 %collective-permute-start.88 = (bf16[768,384]{1,0:T(8,128)(2,1)S(1)}, bf16[768,384]{1,0:T(8,128)(2,1)S(1)}, u32[]{:S(2)}, u32[]{:S(2)}) collective-permute-start(bf16[768,384]{1,0:T(8,128)(2,1)S(1)} %collective-permute-done.84.refs_1_), channel_id=1, source_target_pairs={{4,0},{8,4},{12,8},{14,12},{10,14},{6,10},{2,6},{0,2},{5,1},{9,5},... | collective-permute-start | bytes 1769480 | tf_op jit(solution)/shard_map/ppermute | solution.py:644
  (123 other events, 1003.2 us)
